TPU v7x, 32 devices: a whole 2x2x4 slice. The times are simulated.
32 devices in a mesh: dp: 16 (over z, x, core), head: 2 (over y).
Axes of the slice: x: 2, y: 2, z: 4, core: 2. Of those that a mesh axis runs over, the one named last changes fastest.
Arguments:
- tokens: bfloat16 [16384, 768], P('dp'), may hold values from -6 to 6
- cotangent: bfloat16 [16384, 768], P(('dp', 'head')), may hold values from -6 to 6
- form_number: int32 [16, 1024], P('dp'), may hold values from 0 to 2, never falling along the last dimension, each value on 1 to 709 neighbouring positions
- sequence_bucket: int32 [16384, 1024], P('dp'), may hold values from 0 to 31
- horizontal_bucket: int32 [16384, 1024], P('dp'), may hold values from 0 to 63
- vertical_bucket: int32 [16384, 1024], P('dp'), may hold values from 0 to 63
- project_weight: bfloat16 [768, 3, 768], P(None, None, 'head'), may hold values from -0.21875 to 0.21875
- query_bias: bfloat16 [768], P('head'), may hold values from -3 to 3
- value_bias: bfloat16 [768], P('head'), may hold values from -3 to 3
- output_weight: bfloat16 [768, 768], P('head'), may hold values from -1.75 to 1.75
- output_bias: bfloat16 [768], replicated, may hold values from -3 to 3
- first_gain: bfloat16 [768], replicated, may hold values from 0.5 to 1.5
- first_shift: bfloat16 [768], replicated, may hold values from -2 to 2
- up_weight: bfloat16 [768, 3072], P(None, 'head'), may hold values from -0.21875 to 0.21875
- up_bias: bfloat16 [3072], P('head'), may hold values from -3 to 3
- down_weight: bfloat16 [3072, 768], P('head'), may hold values from -0.109375 to 0.109375
- down_bias: bfloat16 [768], replicated, may hold values from -3 to 3
- second_gain: bfloat16 [768], replicated, may hold values from 0.5 to 1.5
- second_shift: bfloat16 [768], replicated, may hold values from -2 to 2
- sequence_table: bfloat16 [32, 12], P(None, 'head'), may hold values from -4 to 4
- horizontal_table: bfloat16 [64, 12], P(None, 'head'), may hold values from -4 to 4
- vertical_table: bfloat16 [64, 12], P(None, 'head'), may hold values from -4 to 4
- project_weight_average: float32 [768, 3, 768], P('dp', None, 'head'), may hold values from -0.21875 to 0.21875
- query_bias_average: float32 [768], P('head'), may hold values from -3 to 3
- value_bias_average: float32 [768], P('head'), may hold values from -3 to 3
- output_weight_average: float32 [768, 768], P('head', 'dp'), may hold values from -1.75 to 1.75
- output_bias_average: float32 [768], replicated, may hold values from -3 to 3
- first_gain_average: float32 [768], replicated, may hold values from 0.5 to 1.5
- first_shift_average: float32 [768], replicated, may hold values from -2 to 2
- up_weight_average: float32 [768, 3072], P('dp', 'head'), may hold values from -0.21875 to 0.21875
- up_bias_average: float32 [3072], P('head'), may hold values from -3 to 3
- down_weight_average: float32 [3072, 768], P(('head', 'dp')), may hold values from -0.109375 to 0.109375
- down_bias_average: float32 [768], replicated, may hold values from -3 to 3
- second_gain_average: float32 [768], replicated, may hold values from 0.5 to 1.5
- second_shift_average: float32 [768], replicated, may hold values from -2 to 2
- sequence_table_average: float32 [32, 12], P(None, 'head'), may hold values from -4 to 4
- horizontal_table_average: float32 [64, 12], P(None, 'head'), may hold values from -4 to 4
- vertical_table_average: float32 [64, 12], P(None, 'head'), may hold values from -4 to 4
Outputs:
- layer_output: float32 [16384, 768], P(('dp', 'head'))
- tokens_gradient: float32 [16384, 768], P(('dp', 'head'))
- project_weight_gradient: float32 [768, 3, 768], P(None, None, 'head')
- query_bias_gradient: float32 [768], P('head')
- value_bias_gradient: float32 [768], P('head')
- output_weight_gradient: float32 [768, 768], P('head')
- output_bias_gradient: float32 [768], replicated
- first_gain_gradient: float32 [768], replicated
- first_shift_gradient: float32 [768], replicated
- up_weight_gradient: float32 [768, 3072], P(None, 'head')
- up_bias_gradient: float32 [3072], P('head')
- down_weight_gradient: float32 [3072, 768], P('head')
- down_bias_gradient: float32 [768], replicated
- second_gain_gradient: float32 [768], replicated
- second_shift_gradient: float32 [768], replicated
- sequence_table_gradient: float32 [32, 12], P(None, 'head')
- horizontal_table_gradient: float32 [64, 12], P(None, 'head')
- vertical_table_gradient: float32 [64, 12], P(None, 'head')
- project_weight_renewed: float32 [768, 3, 768], P('dp', None, 'head')
- query_bias_renewed: float32 [768], P('head')
- value_bias_renewed: float32 [768], P('head')
- output_weight_renewed: float32 [768, 768], P('head', 'dp')
- output_bias_renewed: float32 [768], replicated
- first_gain_renewed: float32 [768], replicated
- first_shift_renewed: float32 [768], replicated
- up_weight_renewed: float32 [768, 3072], P('dp', 'head')
- up_bias_renewed: float32 [3072], P('head')
- down_weight_renewed: float32 [3072, 768], P(('head', 'dp'))
- down_bias_renewed: float32 [768], replicated
- second_gain_renewed: float32 [768], replicated
- second_shift_renewed: float32 [768], replicated
- sequence_table_renewed: float32 [32, 12], P(None, 'head')
- horizontal_table_renewed: float32 [64, 12], P(None, 'head')
- vertical_table_renewed: float32 [64, 12], P(None, 'head')
Inputs may be any that keep to these rules, and one draw needn't show every extreme that they name: `form_number`: along each pack of 1024 positions the form numbers never fall; a form has at most min(709, 1024) positions, and some form has exactly that many.
All inputs are finite; a program needn't handle non-finite values.
Results may differ from a plain program's by a relative error of at most 0.014.
Values may be sent and summed in bfloat16 or wider, within the bound.
A program may use at most 256 MiB of HBM per device.

v0:
```python
import jax
import jax.numpy as jnp
from jax import lax
from jax.sharding import PartitionSpec as P

norm_epsilon = 1e-05
masked_score = -1e30


def layer_norm(value, gain, shift):
    center = value - jnp.mean(value, axis=-1, keepdims=True)
    spread = jnp.mean(center * center, axis=-1, keepdims=True)
    return center * lax.rsqrt(spread + norm_epsilon) * gain + shift


def exact_gelu(value):
    return jax.nn.gelu(value, approximate=False)


def block_size():
    return 512


def bucket_onehot(bucket, block_start, block_rows, bins):
    picked = bucket[block_start : block_start + block_rows]
    return (picked[:, :, None] == jnp.arange(bins, dtype=jnp.int32)).astype(jnp.bfloat16)


def local(
    tokens,
    cotangent,
    form_number,
    sequence_bucket,
    horizontal_bucket,
    vertical_bucket,
    project_weight,
    query_bias,
    value_bias,
    output_weight,
    output_bias,
    first_gain,
    first_shift,
    up_weight,
    up_bias,
    down_weight,
    down_bias,
    second_gain,
    second_shift,
    sequence_table,
    horizontal_table,
    vertical_table,
    project_weight_average,
    query_bias_average,
    value_bias_average,
    output_weight_average,
    output_bias_average,
    first_gain_average,
    first_shift_average,
    up_weight_average,
    up_bias_average,
    down_weight_average,
    down_bias_average,
    second_gain_average,
    second_shift_average,
    sequence_table_average,
    horizontal_table_average,
    vertical_table_average,
):
    total_rows, model_width = tokens.shape
    local_width = project_weight.shape[2]
    local_heads = sequence_table.shape[1]
    head_width = local_width // local_heads
    share_rows = total_rows // lax.axis_size("head")
    share_start = lax.axis_index("head") * share_rows
    block_rows = block_size()
    starts = list(range(0, total_rows, block_rows))
    form_row = form_number[0]
    buckets = (sequence_bucket, horizontal_bucket, vertical_bucket)
    tables = (sequence_table, horizontal_table, vertical_table)
    flat_project = project_weight.reshape(model_width, 3 * local_width)
    projected = jnp.dot(tokens, flat_project, preferred_element_type=jnp.float32)
    projected = projected.reshape(total_rows, 3, local_width)
    query = ((projected[:, 0] + query_bias.astype(jnp.float32)) * 0.125).astype(jnp.bfloat16)
    query = query.reshape(total_rows, local_heads, head_width)
    key = projected[:, 1].astype(jnp.bfloat16).reshape(total_rows, local_heads, head_width)
    value = (projected[:, 2] + value_bias.astype(jnp.float32)).astype(jnp.bfloat16)
    value = value.reshape(total_rows, local_heads, head_width)
    kept_bias, kept_top, kept_total, context_blocks = ([], [], [], [])
    for block_start in starts:
        block_stop = block_start + block_rows
        bias = jnp.zeros((local_heads, block_rows, total_rows), jnp.float32)
        for bucket, table in zip(buckets, tables):
            onehot = bucket_onehot(bucket, block_start, block_rows, table.shape[0])
            bias = bias + jnp.einsum(
                "qkb,bh->hqk", onehot, table, preferred_element_type=jnp.float32
            )
        same_form = (form_row[block_start:block_stop, None] == form_row[None, :])[None]
        score = (
            jnp.einsum(
                "qhd,khd->hqk",
                query[block_start:block_stop],
                key,
                preferred_element_type=jnp.float32,
            )
            + bias
        )
        score = jnp.where(same_form, score, masked_score)
        top = jnp.max(score, axis=-1, keepdims=True)
        weight = jnp.exp(score - top)
        total = jnp.sum(weight, axis=-1, keepdims=True)
        probs = weight / total
        context_blocks.append(
            jnp.einsum(
                "hqk,khd->qhd",
                probs.astype(jnp.bfloat16),
                value,
                preferred_element_type=jnp.float32,
            )
        )
        kept_bias.append(bias)
        kept_top.append(top)
        kept_total.append(total)
    context = (
        jnp.concatenate(context_blocks, axis=0)
        .reshape(total_rows, local_width)
        .astype(jnp.bfloat16)
    )
    picked = context
    attend = lax.psum_scatter(
        jnp.dot(picked, output_weight, preferred_element_type=jnp.float32),
        "head",
        scatter_dimension=0,
        tiled=True,
    ) + output_bias.astype(jnp.float32)
    own_rows = lax.dynamic_slice_in_dim(tokens, share_start, share_rows, 0).astype(jnp.float32)
    normed, first_pull = jax.vjp(
        layer_norm,
        own_rows + attend,
        first_gain.astype(jnp.float32),
        first_shift.astype(jnp.float32),
    )
    normed_all = lax.all_gather(normed.astype(jnp.bfloat16), "head", axis=0, tiled=True)
    up = jnp.dot(normed_all, up_weight, preferred_element_type=jnp.float32) + up_bias.astype(
        jnp.float32
    )
    act_value, gelu_pull = jax.vjp(exact_gelu, up)
    act = act_value.astype(jnp.bfloat16)
    picked = act
    feed = lax.psum_scatter(
        jnp.dot(picked, down_weight, preferred_element_type=jnp.float32),
        "head",
        scatter_dimension=0,
        tiled=True,
    ) + down_bias.astype(jnp.float32)
    layer_output, second_pull = jax.vjp(
        layer_norm, normed + feed, second_gain.astype(jnp.float32), second_shift.astype(jnp.float32)
    )
    back_second, second_gain_part, second_shift_part = second_pull(cotangent.astype(jnp.float32))
    back_feed = lax.all_gather(back_second.astype(jnp.bfloat16), "head", axis=0, tiled=True)
    down_bias_gradient = jnp.sum(back_feed.astype(jnp.float32), axis=0)
    down_weight_gradient = jnp.einsum(
        "rf,rd->fd", act, back_feed, preferred_element_type=jnp.float32
    )
    back_act = jnp.einsum("rd,fd->rf", back_feed, down_weight, preferred_element_type=jnp.float32)
    back_up = gelu_pull(back_act)[0].astype(jnp.bfloat16)
    up_bias_gradient = jnp.sum(back_up.astype(jnp.float32), axis=0)
    up_weight_gradient = jnp.einsum(
        "rd,rf->df", normed_all, back_up, preferred_element_type=jnp.float32
    )
    feed_sums = None
    picked = back_up
    back_normed = back_second + lax.psum_scatter(
        jnp.einsum("rf,df->rd", picked, up_weight, preferred_element_type=jnp.float32),
        "head",
        scatter_dimension=0,
        tiled=True,
    )
    back_first, first_gain_part, first_shift_part = first_pull(back_normed)
    back_attend = lax.all_gather(back_first.astype(jnp.bfloat16), "head", axis=0, tiled=True)
    output_bias_gradient = jnp.sum(back_attend.astype(jnp.float32), axis=0)
    output_weight_gradient = jnp.einsum(
        "rl,rd->ld", context, back_attend, preferred_element_type=jnp.float32
    )
    back_context = jnp.einsum(
        "rd,ld->rl", back_attend, output_weight, preferred_element_type=jnp.float32
    )
    back_context = back_context.astype(jnp.bfloat16).reshape(total_rows, local_heads, head_width)
    back_key = jnp.zeros((total_rows, local_heads, head_width), jnp.float32)
    back_value = jnp.zeros((total_rows, local_heads, head_width), jnp.float32)
    table_gradients = [jnp.zeros((table.shape[0], local_heads), jnp.float32) for table in tables]
    query_blocks = []
    for index, block_start in enumerate(starts):
        block_stop = block_start + block_rows
        same_form = (form_row[block_start:block_stop, None] == form_row[None, :])[None]
        query_block = query[block_start:block_stop]
        score = (
            jnp.einsum("qhd,khd->hqk", query_block, key, preferred_element_type=jnp.float32)
            + kept_bias[index]
        )
        score = jnp.where(same_form, score, masked_score)
        probs = jnp.exp(score - kept_top[index]) / kept_total[index]
        back_block = back_context[block_start:block_stop]
        back_probs = jnp.einsum(
            "qhd,khd->hqk", back_block, value, preferred_element_type=jnp.float32
        )
        inner = jnp.sum(probs * back_probs, axis=-1, keepdims=True)
        back_score = (probs * (back_probs - inner)).astype(jnp.bfloat16)
        query_blocks.append(
            jnp.einsum("hqk,khd->qhd", back_score, key, preferred_element_type=jnp.float32)
        )
        back_key = back_key + jnp.einsum(
            "hqk,qhd->khd", back_score, query_block, preferred_element_type=jnp.float32
        )
        back_value = back_value + jnp.einsum(
            "hqk,qhd->khd",
            probs.astype(jnp.bfloat16),
            back_block,
            preferred_element_type=jnp.float32,
        )
        for slot in range(3):
            onehot = bucket_onehot(buckets[slot], block_start, block_rows, tables[slot].shape[0])
            table_gradients[slot] = table_gradients[slot] + jnp.einsum(
                "qkb,hqk->bh", onehot, back_score, preferred_element_type=jnp.float32
            )
    back_query = jnp.concatenate(query_blocks, axis=0).astype(jnp.bfloat16) * 0.125
    back_query = back_query.reshape(total_rows, local_width)
    back_key = back_key.astype(jnp.bfloat16).reshape(total_rows, local_width)
    back_value = back_value.astype(jnp.bfloat16).reshape(total_rows, local_width)
    back_project = jnp.stack([back_query, back_key, back_value], axis=1).reshape(
        total_rows, 3 * local_width
    )
    project_weight_gradient = jnp.einsum(
        "rd,rc->dc", tokens, back_project, preferred_element_type=jnp.float32
    )
    project_weight_gradient = project_weight_gradient.reshape(model_width, 3, local_width)
    query_bias_gradient = jnp.sum(back_query.astype(jnp.float32), axis=0)
    value_bias_gradient = jnp.sum(back_value.astype(jnp.float32), axis=0)
    picked = back_project
    tokens_gradient = back_first + lax.psum_scatter(
        jnp.einsum("rc,dc->rd", picked, flat_project, preferred_element_type=jnp.float32).astype(
            jnp.bfloat16
        ),
        "head",
        scatter_dimension=0,
        tiled=True,
    ).astype(jnp.float32)
    norm_sums = lax.psum(
        (first_gain_part, first_shift_part, second_gain_part, second_shift_part), ("dp", "head")
    )
    summed = lax.psum(
        (
            up_weight_gradient,
            up_bias_gradient,
            down_weight_gradient,
            down_bias_gradient,
            project_weight_gradient,
            query_bias_gradient,
            value_bias_gradient,
            output_weight_gradient,
            output_bias_gradient,
            table_gradients[0],
            table_gradients[1],
            table_gradients[2],
        ),
        "dp",
    )
    feed_sums = summed[:4]
    attend_sums = summed[4:]
    up_weight_total, up_bias_total, down_weight_total, down_bias_total = feed_sums
    (
        project_total,
        query_bias_total,
        value_bias_total,
        output_weight_total,
        output_bias_total,
        sequence_total,
        horizontal_total,
        vertical_total,
    ) = attend_sums
    first_gain_total, first_shift_total, second_gain_total, second_shift_total = norm_sums
    token_count = total_rows * lax.axis_size("dp")
    group_count = lax.axis_size("dp")
    group_index = lax.axis_index("dp")

    def renew(average, weight, gradient):
        return 0.5 * average + 0.5 * (weight.astype(jnp.float32) - gradient / token_count)

    def part_of(array, along):
        width = array.shape[along] // group_count
        return lax.dynamic_slice_in_dim(array, group_index * width, width, along)

    return (
        layer_output,
        tokens_gradient,
        project_total,
        query_bias_total,
        value_bias_total,
        output_weight_total,
        output_bias_total,
        first_gain_total,
        first_shift_total,
        up_weight_total,
        up_bias_total,
        down_weight_total,
        down_bias_total,
        second_gain_total,
        second_shift_total,
        sequence_total,
        horizontal_total,
        vertical_total,
        renew(project_weight_average, part_of(project_weight, 0), part_of(project_total, 0)),
        renew(query_bias_average, query_bias, query_bias_total),
        renew(value_bias_average, value_bias, value_bias_total),
        renew(output_weight_average, part_of(output_weight, 1), part_of(output_weight_total, 1)),
        renew(output_bias_average, output_bias, output_bias_total),
        renew(first_gain_average, first_gain, first_gain_total),
        renew(first_shift_average, first_shift, first_shift_total),
        renew(up_weight_average, part_of(up_weight, 0), part_of(up_weight_total, 0)),
        renew(up_bias_average, up_bias, up_bias_total),
        renew(down_weight_average, part_of(down_weight, 0), part_of(down_weight_total, 0)),
        renew(down_bias_average, down_bias, down_bias_total),
        renew(second_gain_average, second_gain, second_gain_total),
        renew(second_shift_average, second_shift, second_shift_total),
        renew(sequence_table_average, sequence_table, sequence_total),
        renew(horizontal_table_average, horizontal_table, horizontal_total),
        renew(vertical_table_average, vertical_table, vertical_total),
    )


def solution(mesh):
    in_specs = (
        P("dp", None),
        P(("dp", "head"), None),
        P("dp", None),
        P("dp", None),
        P("dp", None),
        P("dp", None),
        P(None, None, "head"),
        P("head"),
        P("head"),
        P("head", None),
        P(),
        P(),
        P(),
        P(None, "head"),
        P("head"),
        P("head", None),
        P(),
        P(),
        P(),
        P(None, "head"),
        P(None, "head"),
        P(None, "head"),
        P("dp", None, "head"),
        P("head"),
        P("head"),
        P("head", "dp"),
        P(),
        P(),
        P(),
        P("dp", "head"),
        P("head"),
        P(("head", "dp"), None),
        P(),
        P(),
        P(),
        P(None, "head"),
        P(None, "head"),
        P(None, "head"),
    )
    out_specs = (
        P(("dp", "head"), None),
        P(("dp", "head"), None),
        P(None, None, "head"),
        P("head"),
        P("head"),
        P("head", None),
        P(),
        P(),
        P(),
        P(None, "head"),
        P("head"),
        P("head", None),
        P(),
        P(),
        P(),
        P(None, "head"),
        P(None, "head"),
        P(None, "head"),
        P("dp", None, "head"),
        P("head"),
        P("head"),
        P("head", "dp"),
        P(),
        P(),
        P(),
        P("dp", "head"),
        P("head"),
        P(("head", "dp"), None),
        P(),
        P(),
        P(),
        P(None, "head"),
        P(None, "head"),
        P(None, "head"),
    )
    return jax.shard_map(local, mesh=mesh, in_specs=in_specs, out_specs=out_specs, check_vma=False)
```

profile of v0, /device:TPU:0, one launch (start us, length us, event | category | flops | bytes accessed | tf_op | source)
XLA Modules:
  0.0 1110.5 jit_solution(16827166240045907284)
XLA Ops:
  24.1 22.9 %fusion.3 = f32[512,1024,6]{0,2,1:T(8,128)} fusion(s32[512,1024]{0,1:T(8,128)} %copy.119, bf16[64,6]{0,1:T(8,128)(2,1)S(1)} %copy-done.88), kind=kOutput, calls=%fused_computation.4 | convolution fusion | flops 436207616 | bytes 14680832 | tf_op jit(solution)/shard_map/qkb,bh->hqk/dot_general | solution.py:94
  47.0 15.7 %copy.121 = f32[512,1024,6]{1,0,2:T(8,128)} copy(f32[512,1024,6]{0,2,1:T(8,128)} %fusion.3) | data formatting | bytes 25165824 | tf_op jit(solution)/shard_map/qkb,bh->hqk/dot_general | solution.py:94
  70.4 13.4 %fusion.15 = f32[512,1024,6]{0,2,1:T(8,128)} fusion(s32[512,1024]{0,1:T(8,128)} %copy.113, bf16[32,6]{0,1:T(8,128)(2,1)S(1)} %copy-done.37), kind=kOutput, calls=%fused_computation.20 | convolution fusion | flops 218103808 | bytes 14680448 | tf_op jit(solution)/shard_map/qkb,bh->hqk/dot_general | solution.py:94
  83.8 15.6 %copy.117 = f32[512,1024,6]{1,0,2:T(8,128)} copy(f32[512,1024,6]{0,2,1:T(8,128)} %fusion.15) | data formatting | bytes 25165824 | tf_op jit(solution)/shard_map/qkb,bh->hqk/dot_general | solution.py:94
  107.2 23.1 %fusion.5 = f32[512,1024,6]{0,2,1:T(8,128)} fusion(s32[512,1024]{0,1:T(8,128)} %copy.115, bf16[64,6]{0,1:T(8,128)(2,1)S(1)} %copy-done.90), kind=kOutput, calls=%fused_computation.7 | convolution fusion | flops 436207616 | bytes 14680832 | tf_op jit(solution)/shard_map/qkb,bh->hqk/dot_general | solution.py:94
  130.3 15.7 %copy.118 = f32[512,1024,6]{1,0,2:T(8,128)} copy(f32[512,1024,6]{0,2,1:T(8,128)} %fusion.5) | data formatting | bytes 25165824 | tf_op jit(solution)/shard_map/qkb,bh->hqk/dot_general | solution.py:94
  148.3 18.3 %fusion.26 = f32[6,512,1024]{2,1,0:T(8,128)} fusion(f32[512,1024,6]{1,0,2:T(8,128)} %copy.121, f32[512,1024,6]{1,0,2:T(8,128)} %copy.117, f32[512,1024,6]{1,0,2:T(8,128)} %copy.118, pred[512,1024]{1,0:T(8,128)(4,1)S(1)} %get-tuple-element.149, bf16[512,6,64]{0,2,1:T(8,128)(2,1)S(1)} %bitcast.166, bf16[1024,6,64]{0,2,1:T(8,128)(2,1)S(1)} %bitcast.153), kind=kOutput, calls=%fused_computation.33 | convolution fusion | flops 415236096 | bytes 52035584 | tf_op jit(solution)/shard_map/qhd,khd->hqk/dot_general | solution.py:99
  166.7 15.3 %fusion.95 = (f32[6,512]{1,0:T(8,128)S(1)}, f32[6,512,1024]{2,1,0:T(8,128)}) fusion(f32[6,512,1024]{2,1,0:T(8,128)} %fusion.26), kind=kOutput, calls=%fused_computation.172 | output fusion | flops 6292479 | bytes 25178112 | tf_op jit(solution)/shard_map/sub | solution.py:109
  184.9 22.9 %fusion.7 = f32[512,1024,6]{0,2,1:T(8,128)} fusion(s32[512,1024]{0,1:T(8,128)} %copy.110, bf16[64,6]{0,1:T(8,128)(2,1)S(1)} %copy-done.88), kind=kOutput, calls=%fused_computation.10 | convolution fusion | flops 436207616 | bytes 14680832 | tf_op jit(solution)/shard_map/qkb,bh->hqk/dot_general | solution.py:94
  207.8 16.1 %copy.112 = f32[512,1024,6]{1,0,2:T(8,128)} copy(f32[512,1024,6]{0,2,1:T(8,128)} %fusion.7) | data formatting | bytes 25165824 | tf_op jit(solution)/shard_map/qkb,bh->hqk/dot_general | solution.py:94
  226.8 13.4 %fusion.21 = f32[512,1024,6]{0,2,1:T(8,128)} fusion(s32[512,1024]{0,1:T(8,128)} %copy.104, bf16[32,6]{0,1:T(8,128)(2,1)S(1)} %copy-done.37), kind=kOutput, calls=%fused_computation.27 | convolution fusion | flops 218103808 | bytes 14680448 | tf_op jit(solution)/shard_map/qkb,bh->hqk/dot_general | solution.py:94
  240.2 15.7 %copy.108 = f32[512,1024,6]{1,0,2:T(8,128)} copy(f32[512,1024,6]{0,2,1:T(8,128)} %fusion.21) | data formatting | bytes 25165824 | tf_op jit(solution)/shard_map/qkb,bh->hqk/dot_general | solution.py:94
  258.7 22.9 %fusion.9 = f32[512,1024,6]{0,2,1:T(8,128)} fusion(s32[512,1024]{0,1:T(8,128)} %copy.106, bf16[64,6]{0,1:T(8,128)(2,1)S(1)} %copy-done.90), kind=kOutput, calls=%fused_computation.13 | convolution fusion | flops 436207616 | bytes 14680832 | tf_op jit(solution)/shard_map/qkb,bh->hqk/dot_general | solution.py:94
  281.6 15.7 %copy.109 = f32[512,1024,6]{1,0,2:T(8,128)} copy(f32[512,1024,6]{0,2,1:T(8,128)} %fusion.9) | data formatting | bytes 25165824 | tf_op jit(solution)/shard_map/qkb,bh->hqk/dot_general | solution.py:94
  297.3 18.2 %fusion.27 = f32[6,512,1024]{2,1,0:T(8,128)} fusion(f32[512,1024,6]{1,0,2:T(8,128)} %copy.112, f32[512,1024,6]{1,0,2:T(8,128)} %copy.108, f32[512,1024,6]{1,0,2:T(8,128)} %copy.109, pred[512,1024]{1,0:T(8,128)(4,1)S(1)} %get-tuple-element.148, bf16[512,6,64]{0,2,1:T(8,128)(2,1)S(1)} %bitcast.168, bf16[1024,6,64]{0,2,1:T(8,128)(2,1)S(1)} %bitcast.154), kind=kOutput, calls=%fused_computation.35 | convolution fusion | flops 415236096 | bytes 52035584 | tf_op jit(solution)/shard_map/qhd,khd->hqk/dot_general | solution.py:99
  315.6 15.4 %fusion.96 = (f32[6,512]{1,0:T(8,128)S(1)}, f32[6,512,1024]{2,1,0:T(8,128)}) fusion(f32[6,512,1024]{2,1,0:T(8,128)} %fusion.27), kind=kOutput, calls=%fused_computation.173 | output fusion | flops 6292479 | bytes 25178112 | tf_op jit(solution)/shard_map/sub | solution.py:109
  331.1 14.6 %fusion.61 = bf16[512,6,64]{0,2,1:T(8,128)(2,1)S(1)} fusion(bf16[1024,6,64]{0,2,1:T(8,128)(2,1)S(1)} %add_convert_fusion.3, f32[6,512]{1,0:T(8,128)S(1)} %get-tuple-element.152, f32[6,512,1024]{2,1,0:T(8,128)} %fusion.26), kind=kOutput, calls=%fused_computation.114 | convolution fusion | flops 412291072 | bytes 13774848 | tf_op jit(solution)/shard_map/hqk,khd->qhd/dot_general | solution.py:113
  345.7 14.4 %fusion.64 = bf16[512,6,64]{0,2,1:T(8,128)(2,1)S(1)} fusion(bf16[1024,6,64]{0,2,1:T(8,128)(2,1)S(1)} %add_convert_fusion.3, f32[6,512]{1,0:T(8,128)S(1)} %get-tuple-element.154, f32[6,512,1024]{2,1,0:T(8,128)} %fusion.27), kind=kOutput, calls=%fused_computation.115 | convolution fusion | flops 412291072 | bytes 13774848 | tf_op jit(solution)/shard_map/hqk,khd->qhd/dot_general | solution.py:113
  364.0 46.1 %reduce-scatter.5.cloned.1.call-done = f32[512,768]{1,0:T(8,128)} async-done(((f32[1024,768]{1,0:T(8,128)}), f32[512,768]{1,0:T(8,128)}) %reduce-scatter.5.cloned.1.call-update) | async-done | bytes 1572880 | tf_op jit(solution)/shard_map/reduce_scatter | solution.py:129
  413.6 27.3 %all-gather.4.cloned.1.call-done = bf16[1024,768]{1,0:T(8,128)(2,1)} async-done(((bf16[512,768]{1,0:T(8,128)(2,1)}), bf16[1024,768]{1,0:T(8,128)(2,1)}) %all-gather.4.cloned.1.call-update) | async-done | bytes 1572880 | tf_op jit(solution)/shard_map/all_gather | solution.py:142
  440.9 20.0 %multiply_convert_fusion.2 = (bf16[1024,1536]{1,0:T(8,128)(2,1)S(1)}, f32[1024,1536]{1,0:T(8,128)}, f32[1024,1536]{1,0:T(8,128)}) fusion(f32[1536]{0:T(1024)S(1)} %convert_element_type.179, bf16[1024,768]{1,0:T(8,128)(2,1)} %all-gather.4.cloned.1.call-done, bf16[768,1536]{1,0:T(8,128)(2,1)} %param.51), kind=kOutput, calls=%fused_computation.46 | convolution fusion | flops 2519728128 | bytes 19666944 | tf_op jit(solution)/shard_map/dot_general | solution.py:143
  470.7 39.6 %reduce-scatter.7.cloned.1.call-done = f32[512,768]{1,0:T(8,128)} async-done(((f32[1024,768]{1,0:T(8,128)}), f32[512,768]{1,0:T(8,128)}) %reduce-scatter.7.cloned.1.call-update) | async-done | bytes 1572880 | tf_op jit(solution)/shard_map/reduce_scatter | solution.py:149
  518.2 27.1 %all-gather.6.cloned.1.call-done = bf16[1024,768]{1,0:T(8,128)(2,1)} async-done(((bf16[512,768]{1,0:T(8,128)(2,1)}), bf16[1024,768]{1,0:T(8,128)(2,1)}) %all-gather.6.cloned.1.call-update) | async-done | bytes 1572880 | tf_op jit(solution)/shard_map/all_gather | solution.py:159
  562.3 43.4 %reduce-scatter.9.cloned.1.call-done = f32[512,768]{1,0:T(8,128)} async-done(((f32[1024,768]{1,0:T(8,128)}), f32[512,768]{1,0:T(8,128)}) %reduce-scatter.9.cloned.1.call-update) | async-done | bytes 1572880 | tf_op jit(solution)/shard_map/reduce_scatter | solution.py:172
  620.0 19.2 %all-gather.8.cloned.1.call-done = bf16[1024,768]{1,0:T(8,128)(2,1)} async-done(((bf16[512,768]{1,0:T(8,128)(2,1)}), bf16[1024,768]{1,0:T(8,128)(2,1)}) %all-gather.8.cloned.1.call-update) | async-done | bytes 1572880 | tf_op jit(solution)/shard_map/all_gather | solution.py:179
  727.5 40.0 %all-reduce = (f32[768]{0:T(1024)S(1)}, f32[768]{0:T(1024)S(1)}, f32[768]{0:T(1024)S(1)}, f32[768]{0:T(1024)S(1)}) all-reduce(f32[768]{0:T(1024)S(1)} %copy-done.48, f32[768]{0:T(1024)S(1)} %copy-done.49, f32[768]{0:T(1024)S(1)} %copy-done.43, f32[768]{0:T(1024)S(1)} %copy-done.44), channel_id=1, replica_groups=mesh['dp'=16,'head'=2] {'dp','head'}, use_global_device_ids=true, to_apply=%region_27.28 | all-reduce | flops 3072 | bytes 24576 | tf_op jit(solution)/shard_map/psum | solution.py:247
  840.3 21.9 %fusion.69 = f32[64,6]{0,1:T(8,128)S(1)} fusion(bf16[6,512,1024]{1,0,2:T(8,128)(2,1)S(1)} %bitcast.160, s32[512,1024]{0,1:T(8,128)} %copy.106), kind=kOutput, calls=%fused_computation.118 | convolution fusion | flops 436207616 | bytes 8390144 | tf_op jit(solution)/shard_map/qkb,hqk->bh/dot_general | solution.py:222
  862.2 22.8 %fusion.70 = f32[64,6]{0,1:T(8,128)S(1)} fusion(bf16[6,512,1024]{1,0,2:T(8,128)(2,1)} %copy.128, s32[512,1024]{0,1:T(8,128)S(1)} %copy-done.17), kind=kOutput, calls=%fused_computation.119 | convolution fusion | flops 436207616 | bytes 8390144 | tf_op jit(solution)/shard_map/qkb,hqk->bh/dot_general | solution.py:222
  885.1 20.8 %fusion.74 = f32[64,6]{0,1:T(8,128)S(1)} fusion(f32[64,6]{0,1:T(8,128)S(1)} %fusion.69, bf16[6,512,1024]{1,0,2:T(8,128)(2,1)S(1)} %bitcast.158, s32[512,1024]{0,1:T(8,128)S(1)} %copy-done.16), kind=kOutput, calls=%fused_computation.123 | convolution fusion | flops 436208000 | bytes 8391680 | tf_op jit(solution)/shard_map/qkb,hqk->bh/dot_general | solution.py:222
  906.1 21.0 %fusion.73 = f32[64,6]{0,1:T(8,128)S(1)} fusion(f32[64,6]{0,1:T(8,128)S(1)} %fusion.70, bf16[6,512,1024]{1,0,2:T(8,128)(2,1)S(1)} %bitcast.158, s32[512,1024]{0,1:T(8,128)S(1)} %copy-done.15), kind=kOutput, calls=%fused_computation.122 | convolution fusion | flops 436208000 | bytes 8391680 | tf_op jit(solution)/shard_map/qkb,hqk->bh/dot_general | solution.py:222
  927.1 62.0 %all-reduce.1 = (f32[384]{0:T(512)S(1)}, f32[384]{0:T(512)S(1)}, f32[768]{0:T(1024)S(1)}, f32[1536]{0:T(1024)S(1)}, f32[768]{0:T(1024)S(1)}, /*index=5*/f32[32,6...) all-reduce(f32[384]{0:T(512)S(1)} %convert_reduce_fusion.5, ...), channel_id=1, replica_groups=mesh['dp'=16,'head'=2] {'dp'}, use_global_device_ids=true, to_apply=%region_20.21 | all-reduce | flops 4800 | bytes 38400 | tf_op jit(solution)/shard_map/psum | solution.py:250
  994.9 90.3 %all-reduce.5.cloned.1.call-done = (f32[768,3,384]{2,0,1:T(8,128)}, f32[384,768]{1,0:T(8,128)}, f32[768,1536]{1,0:T(8,128)}, f32[1536,768]{1,0:T(8,128)}) async-done(((f32[768,3,384]{2,0,1:T(8,128)}, f32[384,768]{1,0:T(8,128)}, f32[768,1536]{1,0:T(8,128)}, f32[1536,768]{1,0:T(8,128)}), (f32[768,3,384]{2,0,1:T(8,128)}, f32[384,768]{1,0:T(8,128)}, f32[768,1536]{1,0:T(8,128)}, ...) | async-done | bytes 14155792 | tf_op jit(solution)/shard_map/psum | solution.py:250
  (348 shorter events, 284.3 us)
Async XLA Ops:
  7.2 402.9 %reduce-scatter.5.cloned.1.call-start = ((), (), s32[]{:S(2)}) async-start(), calls=%async_computation.4 | async-start | bytes 4718592 | tf_op jit(solution)/shard_map/reduce_scatter | solution.py:129
  181.9 149.2 %copy-start.30 = (f32[6,512]{1,0:T(8,128)}, f32[6,512]{1,0:T(8,128)S(1)}, u32[]{:S(2)}) copy-start(f32[6,512]{1,0:T(8,128)S(1)} %get-tuple-element.152) | copy-start | bytes 36868
  363.9 77.0 %all-gather.4.cloned.1.call-start = ((), (), s32[]{:S(2)}) async-start(), calls=%async_computation.5 | async-start | bytes 2359296 | tf_op jit(solution)/shard_map/all_gather | solution.py:142
  413.5 96.8 %reduce-scatter.7.cloned.1.call-start = ((), (), s32[]{:S(2)}) async-start(), calls=%async_computation.6 | async-start | bytes 4718592 | tf_op jit(solution)/shard_map/reduce_scatter | solution.py:149
  466.8 78.5 %all-gather.6.cloned.1.call-start = ((), (), s32[]{:S(2)}) async-start(), calls=%async_computation.7 | async-start | bytes 2359296 | tf_op jit(solution)/shard_map/all_gather | solution.py:159
  517.9 87.8 %reduce-scatter.9.cloned.1.call-start = ((), (), s32[]{:S(2)}) async-start(), calls=%async_computation.8 | async-start | bytes 4718592 | tf_op jit(solution)/shard_map/reduce_scatter | solution.py:172
  562.2 77.1 %all-gather.8.cloned.1.call-start = ((), (), s32[]{:S(2)}) async-start(), calls=%async_computation.9 | async-start | bytes 2359296 | tf_op jit(solution)/shard_map/all_gather | solution.py:179
  611.9 380.3 %reduce-scatter.11.cloned.1.call-start = ((), (), s32[]{:S(2)}) async-start(), calls=%async_computation.10 | async-start | bytes 2359296 | tf_op jit(solution)/shard_map/reduce_scatter | solution.py:239
  718.3 366.8 %all-reduce.5.cloned.1.call-start = ((), (), s32[]{:S(2)}) async-start(), calls=%async_computation.11 | async-start | bytes 28311552 | tf_op jit(solution)/shard_map/psum | solution.py:250
  906.0 84.4 %copy-start.46 = (bf16[1536]{0:T(1024)(128)(2,1)S(1)}, bf16[1536]{0:T(1024)(128)(2,1)}, u32[]{:S(2)}) copy-start(bf16[1536]{0:T(1024)(128)(2,1)} %param.52) | copy-start | bytes 9220
  906.0 85.0 %copy-start.59 = (bf16[768]{0:T(1024)(128)(2,1)S(1)}, bf16[768]{0:T(1024)(128)(2,1)}, u32[]{:S(2)}) copy-start(bf16[768]{0:T(1024)(128)(2,1)} %param.48) | copy-start | bytes 4612
  906.0 85.0 %copy-start.60 = (bf16[768]{0:T(1024)(128)(2,1)S(1)}, bf16[768]{0:T(1024)(128)(2,1)}, u32[]{:S(2)}) copy-start(bf16[768]{0:T(1024)(128)(2,1)} %param.54) | copy-start | bytes 4612
  906.0 85.0 %copy-start.74 = (f32[768]{0:T(1024)S(1)}, f32[768]{0:T(1024)}, u32[]{:S(2)}) copy-start(f32[768]{0:T(1024)} %param.70) | copy-start | bytes 9220
  906.0 85.0 %copy-start.75 = (f32[768]{0:T(1024)S(1)}, f32[768]{0:T(1024)}, u32[]{:S(2)}) copy-start(f32[768]{0:T(1024)} %param.64) | copy-start | bytes 9220
  906.0 85.6 %copy-start.76 = (f32[64,6]{0,1:T(8,128)S(1)}, f32[64,6]{0,1:T(8,128)}, u32[]{:S(2)}) copy-start(f32[64,6]{0,1:T(8,128)} %param.75) | copy-start | bytes 4612
  906.0 85.6 %copy-start.77 = (f32[64,6]{0,1:T(8,128)S(1)}, f32[64,6]{0,1:T(8,128)}, u32[]{:S(2)}) copy-start(f32[64,6]{0,1:T(8,128)} %param.74) | copy-start | bytes 4612
  906.1 85.6 %copy-start.89 = (bf16[64,6]{0,1:T(8,128)(2,1)S(1)}, bf16[64,6]{0,1:T(8,128)(2,1)}, u32[]{:S(2)}) copy-start(bf16[64,6]{0,1:T(8,128)(2,1)} %param.59) | copy-start | bytes 2308
  906.1 85.6 %copy-start.91 = (bf16[64,6]{0,1:T(8,128)(2,1)S(1)}, bf16[64,6]{0,1:T(8,128)(2,1)}, u32[]{:S(2)}) copy-start(bf16[64,6]{0,1:T(8,128)(2,1)} %param.58) | copy-start | bytes 2308
  906.1 86.2 %copy-start.3 = (f32[512,768]{1,0:T(8,128)S(1)}, f32[512,768]{1,0:T(8,128)}, u32[]{:S(2)}) copy-start(f32[512,768]{1,0:T(8,128)} %copy-done.2) | copy-start | bytes 4718596
  906.1 86.2 %copy-start.36 = (f32[512]{0:T(512)S(1)}, f32[512]{0:T(512)}, u32[]{:S(2)}) copy-start(f32[512]{0:T(512)} %copy-done.35) | copy-start | bytes 6148
  906.1 179.1 %copy-start.23 = (f32[384,48]{1,0:T(8,128)S(1)}, f32[384,48]{1,0:T(8,128)}, u32[]{:S(2)}) copy-start(f32[384,48]{1,0:T(8,128)} %copy.134) | copy-start | bytes 221188
  906.1 181.1 %copy-start.28 = (f32[48,3,384]{2,0,1:T(8,128)S(1)}, f32[48,3,384]{2,0,1:T(8,128)}, u32[]{:S(2)}) copy-start(f32[48,3,384]{2,0,1:T(8,128)} %param.60) | copy-start | bytes 663556
  906.1 182.8 %copy-start.26 = (f32[48,1536]{1,0:T(8,128)S(1)}, f32[48,1536]{1,0:T(8,128)}, u32[]{:S(2)}) copy-start(f32[48,1536]{1,0:T(8,128)} %param.67) | copy-start | bytes 884740
  927.1 163.6 %copy-start.27 = (f32[96,768]{1,0:T(8,128)S(1)}, f32[96,768]{1,0:T(8,128)}, u32[]{:S(2)}) copy-start(f32[96,768]{1,0:T(8,128)} %param.69) | copy-start | bytes 884740
  989.1 107.6 %copy-start.62 = (f32[1536]{0:T(1024)}, f32[1536]{0:T(1024)S(1)}, u32[]{:S(2)}) copy-start(f32[1536]{0:T(1024)S(1)} %get-tuple-element.183) | copy-start | bytes 18436
  989.1 107.6 %copy-start.82 = (f32[768]{0:T(1024)}, f32[768]{0:T(1024)S(1)}, u32[]{:S(2)}) copy-start(f32[768]{0:T(1024)S(1)} %get-tuple-element.179) | copy-start | bytes 9220
  989.1 107.6 %copy-start.83 = (f32[768]{0:T(1024)}, f32[768]{0:T(1024)S(1)}, u32[]{:S(2)}) copy-start(f32[768]{0:T(1024)S(1)} %get-tuple-element.185) | copy-start | bytes 9220
  989.1 107.6 %copy-start.84 = (f32[32,6]{0,1:T(8,128)}, f32[32,6]{0,1:T(8,128)S(1)}, u32[]{:S(2)}) copy-start(f32[32,6]{0,1:T(8,128)S(1)} %get-tuple-element.188) | copy-start | bytes 2308
  989.1 107.6 %copy-start.85 = (f32[64,6]{0,1:T(8,128)}, f32[64,6]{0,1:T(8,128)S(1)}, u32[]{:S(2)}) copy-start(f32[64,6]{0,1:T(8,128)S(1)} %get-tuple-element.189) | copy-start | bytes 4612
  989.1 107.6 %copy-start.86 = (f32[64,6]{0,1:T(8,128)}, f32[64,6]{0,1:T(8,128)S(1)}, u32[]{:S(2)}) copy-start(f32[64,6]{0,1:T(8,128)S(1)} %get-tuple-element.190) | copy-start | bytes 4612
  989.1 107.6 %copy-start.94 = (f32[384]{0:T(512)}, f32[384]{0:T(512)S(1)}, u32[]{:S(2)}) copy-start(f32[384]{0:T(512)S(1)} %get-tuple-element.176) | copy-start | bytes 4612
  989.2 107.6 %copy-start.95 = (f32[384]{0:T(512)}, f32[384]{0:T(512)S(1)}, u32[]{:S(2)}) copy-start(f32[384]{0:T(512)S(1)} %get-tuple-element.177) | copy-start | bytes 4612
  (88 other events, 1994.1 us)
Sparse Core Ops, SparseCore 0:
  364.0 46.0 reduce-scatter.4
  413.6 27.2 all-gather.3
  466.9 43.3 reduce-scatter.6
  518.0 27.2 all-gather.5
  562.3 43.3 reduce-scatter.8
  612.0 27.2 all-gather.7
  718.5 26.7 reduce-scatter.10
  824.9 260.1 all-reduce.4
where the time goes:
time: 1120 us; the launch traced here: 1110 us
  matrix products  427 us (38%)
  waiting for transfers between devices  293 us (26%)
  local copies, waits for them, and re-layouts  189 us (17%)
  blocking collectives  102 us (9%)
  other arithmetic  82.9 us (7%)
  between operations  15.6 us (1%)
    dot_general x6, matrix products, local(): jnp.einsum('qkb,bh->hqk', onehot, table, preferred_element_type=jnp.float32)  119 us
    dot_general x6, matrix products, local(): jnp.einsum('qkb,hqk->bh', onehot, back_score, preferred_element_type=jnp....  112 us
    dot_general x6, local copies, waits for them, and re-layouts, local(): jnp.einsum('qkb,bh->hqk', onehot, table, preferred_element_type=jnp.float32)  94.4 us
    psum x1, waiting for transfers between devices, local(): lax.psum((up_weight_gradient, up_bias_gradient, down_weight_gradient, dow...  90.3 us
    psum x1, blocking collectives, local(): lax.psum((up_weight_gradient, up_bias_gradient, down_weight_gradient, dow...  62 us
    reduce_scatter x1, waiting for transfers between devices, local(): lax.psum_scatter(jnp.dot(picked, output_weight, preferred_element_type=jn...  46.1 us
    reduce_scatter x1, waiting for transfers between devices, local(): lax.psum_scatter(jnp.einsum('rf,df->rd', picked, up_weight, preferred_ele...  43.4 us
    psum x1, blocking collectives, local(): lax.psum((first_gain_part, first_shift_part, second_gain_part, second_shi...  40 us
  transfers between devices with their start and end apart: 8, of which 7 were waited for; matrix products, arithmetic and copies ran while one was open for 17% of the time, Pallas kernels for 0%

commit v1 on v0

v1 whole, which is shorter than its diff:
```python
import functools
import jax
import jax.numpy as jnp
from jax import lax
from jax.experimental import pallas as pl
from jax.sharding import PartitionSpec as P
from jax.experimental.pallas import tpu as pltpu

F32, BF16, I32 = jnp.float32, jnp.bfloat16, jnp.int32
SCALE_BITS = 27
STEP = 2.0**11
VM = 56 * 2**20


def dot_nt(a, b):
    return lax.dot_general(a, b, (((1,), (1,)), ((), ())), preferred_element_type=F32)


def dot_tn(a, b):
    return lax.dot_general(a, b, (((0,), (0,)), ((), ())), preferred_element_type=F32)


def dot_general_t(w, x):
    return lax.dot_general(w, x, (((0,), (1,)), ((), ())), preferred_element_type=F32)


def dot_tt(a, b):
    return lax.dot_general(a, b, (((0,), (1,)), ((), ())), preferred_element_type=F32)


def dot_nn(a, b):
    return lax.dot_general(a, b, (((1,), (0,)), ((), ())), preferred_element_type=F32)


def split_pair(x):
    lane = lax.broadcasted_iota(I32, x.shape, 1)
    zero = jnp.zeros_like(x)
    return jnp.concatenate([jnp.where(lane < 64, x, zero), jnp.where(lane < 64, zero, x)], axis=0)


def fwd_kernel(off, seq, hor, ver, formc, formr, tab, q, kt, v, p_out, c_out, b_ref, *, pairs, qb):
    keys = v.shape[0]
    chunk = 128
    tbs = [jnp.broadcast_to(tab[i : i + 1, :], (8, chunk)) for i in range(3 * pairs)]

    def gather(r, _):
        rs = pl.ds(pl.multiple_of(r * 8, 8), 8)
        for c in range(keys // chunk):
            ls = slice(c * chunk, (c + 1) * chunk)
            sums = [None] * pairs
            for t, b in enumerate((seq, hor, ver)):
                idx = b[rs, ls]
                for j in range(pairs):
                    g = jnp.take_along_axis(tbs[3 * j + t], idx, axis=1, mode="promise_in_bounds")
                    sums[j] = g if t == 0 else sums[j] + g
            for j in range(pairs):
                b_ref[j, rs, ls] = sums[j]
        return 0

    lax.fori_loop(0, qb // 8, gather, 0)
    same = formc[...] == formr[...]
    for j in range(pairs):
        lanes = slice(j * 128, (j + 1) * 128)
        q2 = split_pair(q[:, lanes])
        s2 = dot_nn(q2, kt[lanes, :])
        bias = b_ref[j]
        for g in range(2):
            x = s2[g * qb : (g + 1) * qb] + (bias << 16 if g else bias).astype(F32)
            x = jnp.where(same, x, -1e30)
            top = jnp.max(x, axis=1, keepdims=True)
            e = jnp.exp2((x - top) * (1.4426950408889634 * 2.0**-SCALE_BITS))
            inv = 1.0 / jnp.sum(e, axis=1, keepdims=True)
            p_out[2 * j + g] = (e * inv).astype(BF16)
        c0 = dot_nn(p_out[2 * j], v[:, lanes])
        c1 = dot_nn(p_out[2 * j + 1], v[:, lanes])
        lane = lax.broadcasted_iota(I32, c0.shape, 1)
        c_out[:, lanes] = jnp.where(lane < 64, c0, c1).astype(BF16)


def attend_fwd(off, buckets, formc, formr, tab, q, kt, v, qb=128):
    nq, width = q.shape
    keys = v.shape[0]
    pairs = width // 128
    bspec = pl.BlockSpec((qb, keys), lambda i, off: (i + off[0], 0))
    full = lambda a: pl.BlockSpec(a.shape, lambda i, off: (0,) * a.ndim)
    return pl.pallas_call(
        functools.partial(fwd_kernel, pairs=pairs, qb=qb),
        out_shape=(
            jax.ShapeDtypeStruct((2 * pairs, nq, keys), BF16),
            jax.ShapeDtypeStruct((nq, width), BF16),
        ),
        grid_spec=pltpu.PrefetchScalarGridSpec(
            num_scalar_prefetch=1,
            grid=(nq // qb,),
            in_specs=[bspec] * 3
            + [
                pl.BlockSpec((qb, 1), lambda i, off: (i + off[0], 0)),
                full(formr),
                full(tab),
                pl.BlockSpec((qb, width), lambda i, off: (i, 0)),
                full(kt),
                full(v),
            ],
            out_specs=(
                pl.BlockSpec((2 * pairs, qb, keys), lambda i, off: (0, i, 0)),
                pl.BlockSpec((qb, width), lambda i, off: (i, 0)),
            ),
            scratch_shapes=[pltpu.VMEM((pairs, qb, keys), I32)],
        ),
        compiler_params=pltpu.CompilerParams(vmem_limit_bytes=VM),
        cost_estimate=pl.CostEstimate(
            flops=4 * nq * keys * width, bytes_accessed=16 * 2**20, transcendentals=nq * keys * 2 * pairs
        ),
    )(off, *buckets, formc, formr, tab, q, kt, v)


def bwd_kernel(q, k, vt, do, p, ds_out, dq_out, dk_out, dv_out, *, pairs, qb):
    keys = k.shape[0]

    @pl.when(pl.program_id(0) == 0)
    def _():
        dk_out[...] = jnp.zeros_like(dk_out)
        dv_out[...] = jnp.zeros_like(dv_out)

    for j in range(pairs):
        lanes = slice(j * 128, (j + 1) * 128)
        q2 = split_pair(q[:, lanes])
        do2 = split_pair(do[:, lanes])
        dp2 = dot_nn(do2, vt[lanes, :])

        for g in range(2):
            ps = p[2 * j + g].astype(F32)
            ts = ps * dp2[g * qb : (g + 1) * qb]
            inner = jnp.sum(ts, axis=1, keepdims=True)
            ds_out[2 * j + g] = (ts - ps * inner).astype(BF16)
        d0 = dot_nn(ds_out[2 * j], k[:, lanes])
        d1 = dot_nn(ds_out[2 * j + 1], k[:, lanes])
        lane = lax.broadcasted_iota(I32, d0.shape, 1)
        dq_out[:, lanes] = jnp.where(lane < 64, d0, d1).astype(BF16) * jnp.array(0.125, BF16)
        ds2 = ds_out[2 * j : 2 * j + 2].reshape(2 * qb, keys)
        p2 = p[2 * j : 2 * j + 2].reshape(2 * qb, keys)
        dk_out[lanes, :] += dot_tn(q2, ds2)
        dv_out[lanes, :] += dot_tn(do2, p2)


def attend_bwd(q, k, vt, do, p, qb=128):
    nq, width = q.shape
    keys = k.shape[0]
    pairs = width // 128
    full = lambda a: pl.BlockSpec(a.shape, lambda i: (0,) * a.ndim)
    row = pl.BlockSpec((qb, width), lambda i: (i, 0))
    big = pl.BlockSpec((2 * pairs, qb, keys), lambda i: (0, i, 0))
    acc = pl.BlockSpec((width, keys), lambda i: (0, 0))
    return pl.pallas_call(
        functools.partial(bwd_kernel, pairs=pairs, qb=qb),
        out_shape=(
            jax.ShapeDtypeStruct((2 * pairs, nq, keys), BF16),
            jax.ShapeDtypeStruct((nq, width), BF16),
            jax.ShapeDtypeStruct((width, keys), F32),
            jax.ShapeDtypeStruct((width, keys), F32),
        ),
        grid=(nq // qb,),
        in_specs=[row, full(k), full(vt), row, big],
        out_specs=(big, row, acc, acc),
        compiler_params=pltpu.CompilerParams(vmem_limit_bytes=VM),
        cost_estimate=pl.CostEstimate(
            flops=8 * nq * keys * width, bytes_accessed=30 * 2**20, transcendentals=0
        ),
    )(q, k, vt, do, p)


def hist_kernel(off, seq, hor, ver, dsa, dsb, seq_out, hor_out, ver_out, rhs_ref, *, qb, bits):
    keys = seq.shape[1]
    heads = (dsa.shape[0], dsb.shape[0])
    nh = sum(heads)
    outs = (seq_out, hor_out, ver_out)

    @pl.when(pl.program_id(0) == 0)
    def _():
        for o in outs:
            o[...] = jnp.zeros_like(o)

    def rows(r, _):
        rs = pl.ds(pl.multiple_of(r * 16, 16), 16)
        dfull = [d[h, rs, :].astype(F32) for d, n in ((dsa, heads[0]), (dsb, heads[1])) for h in range(n)]
        for half in range(2):
            d8 = [d[half * 8 : half * 8 + 8] for d in dfull]
            for t, b in enumerate((seq, hor, ver)):
                idx = b[pl.ds(pl.multiple_of(r * 16 + half * 8, 8), 8), :]
                signs = [(((idx << (31 - i)) >> 31) | 1).astype(F32) for i in range(bits[t])]
                rhs = jnp.concatenate(
                    [jnp.concatenate([d, d * signs[0]], axis=0).astype(BF16) for d in d8], axis=0
                )
                first = jnp.concatenate([jnp.ones_like(signs[1]), signs[1]], axis=0).astype(BF16)
                tiles = [first]
                for i in range(2, bits[t]):
                    s2 = jnp.concatenate([signs[i], signs[i]], axis=0).astype(BF16)
                    tiles = tiles + [x * s2 for x in tiles]
                lhs = jnp.concatenate(tiles, axis=0)
                outs[t][...] += dot_nt(lhs, rhs)
        return 0

    lax.fori_loop(0, qb // 16, rows, 0)


def hist(off, buckets, dsa, dsb, bits, qb=128):
    nq, keys = dsa.shape[1], dsa.shape[2]
    nh = dsa.shape[0] + dsb.shape[0]
    bspec = pl.BlockSpec((qb, keys), lambda i, off: (i + off[0], 0))
    shapes = [(2 ** (b - 1) * 8, nh * 16) for b in bits]
    return pl.pallas_call(
        functools.partial(hist_kernel, qb=qb, bits=bits),
        out_shape=tuple(jax.ShapeDtypeStruct(s, F32) for s in shapes),
        grid_spec=pltpu.PrefetchScalarGridSpec(
            num_scalar_prefetch=1,
            grid=(nq // qb,),
            in_specs=[bspec] * 3
            + [pl.BlockSpec((d.shape[0], qb, keys), lambda i, off: (0, i, 0)) for d in (dsa, dsb)],
            out_specs=tuple(pl.BlockSpec(s, lambda i, off: (0, 0)) for s in shapes),
            scratch_shapes=[pltpu.VMEM((nh * 16, keys), BF16)],
        ),
        compiler_params=pltpu.CompilerParams(vmem_limit_bytes=VM),
        cost_estimate=pl.CostEstimate(
            flops=2 * nq * keys * 160 * nh * 8, bytes_accessed=20 * 2**20, transcendentals=0
        ),
    )(off, *buckets, dsa, dsb)


def unhist(acc, bits, nh):
    n = 2**bits
    a = acc.reshape(n // 2, 8, nh, 2, 8)
    m = jnp.einsum("fqhvq->fhv", a)
    b = jnp.arange(n)
    sign = lambda i: 1.0 - 2.0 * ((b >> i) & 1).astype(F32)
    tiles = [jnp.stack([jnp.ones((n,), F32), sign(1)])]
    for i in range(2, bits):
        tiles = tiles + [x * sign(i)[None] for x in tiles]
    lhs = jnp.concatenate(tiles)
    var = jnp.stack([jnp.ones((n,), F32), sign(0)])
    return jnp.einsum("fhv,fb,vb->bh", m, lhs, var, precision=lax.Precision.HIGHEST) / n


def pack_tables(tables):
    rows = [jnp.pad(t.astype(F32).T, ((0, 0), (0, 128 - t.shape[0]))) for t in tables]
    fixed = jnp.round(jnp.stack(rows, axis=1) * STEP).astype(I32)
    fixed = fixed.reshape(fixed.shape[0] // 2, 2, 3, 128)
    return (fixed[:, 0] * 65536 + fixed[:, 1]).reshape(-1, 128)


norm_epsilon = 1e-05


def mm(a, b):
    return jnp.dot(a, b, preferred_element_type=F32)


def normalize(value):
    center = value - jnp.mean(value, axis=-1, keepdims=True)
    spread = jnp.mean(center * center, axis=-1, keepdims=True)
    root = lax.rsqrt(spread + norm_epsilon)
    return center * root, root


def normalize_back(grad, normed, root):
    return root * (
        grad
        - jnp.mean(grad, axis=-1, keepdims=True)
        - normed * jnp.mean(grad * normed, axis=-1, keepdims=True)
    )


def gelu_parts(u):
    t = 1.0 / (1.0 + (0.3275911 * 0.7071067811865476) * jnp.abs(u))
    e = jnp.exp(-0.5 * u * u)
    poly = t * (
        0.254829592 + t * (-0.284496736 + t * (1.421413741 + t * (-1.453152027 + t * 1.061405429)))
    )
    tail = 0.5 * e * poly
    below = jnp.where(u >= 0, 1.0 - tail, tail)
    return u * below, below + u * (e * 0.3989422804014327)


def swap_dp(x, bit):
    n = lax.axis_size("dp")
    return lax.ppermute(x, "dp", [(i, i ^ bit) for i in range(n)])


def swap_head(x):
    return lax.ppermute(x, "head", [(0, 1), (1, 0)])


def dp_bits():
    n, bit, out = lax.axis_size("dp"), 1, []
    while bit < n:
        out.append(bit)
        bit *= 2
    return out


def bit_of(bit):
    return (lax.axis_index("dp") // bit) % 2


def in_order(first, mine, theirs):
    low = jnp.where(first == 0, mine, theirs)
    high = jnp.where(first == 0, theirs, mine)
    return jnp.concatenate([low, high], axis=0)


def rows_of(x, index, rows):
    return lax.dynamic_slice_in_dim(x, index * rows, rows, 0)


def fetch_other(w):
    rows = w.shape[0] // 4
    c, x = bit_of(1), bit_of(2)
    mine = swap_head(rows_of(w, 2 * c + x, rows))
    half = in_order(x, mine, swap_dp(mine, 2))
    return in_order(c, half, swap_dp(half, 1))


def halve(g, bit):
    rows = g.shape[0] // 2
    b = bit_of(bit)
    got = swap_dp(rows_of(g, 1 - b, rows), bit)
    return (rows_of(g, b, rows).astype(F32) + got.astype(F32)).astype(BF16)


def reduce_grad(own, other, head_first):
    bits = dp_bits()
    own, other = halve(own, 1), halve(other, 1)
    if not head_first:
        own, other = halve(own, 2), halve(other, 2)
    g = (own.astype(F32) + swap_head(other).astype(F32)).astype(BF16)
    for bit in bits[1 if head_first else 2 :]:
        g = halve(g, bit)
    for bit in reversed(bits):
        g = in_order(bit_of(bit), g, swap_dp(g, bit))
    return g.astype(F32)


def local(
    tokens,
    cotangent,
    form_number,
    sequence_bucket,
    horizontal_bucket,
    vertical_bucket,
    project_weight,
    query_bias,
    value_bias,
    output_weight,
    output_bias,
    first_gain,
    first_shift,
    up_weight,
    up_bias,
    down_weight,
    down_bias,
    second_gain,
    second_shift,
    sequence_table,
    horizontal_table,
    vertical_table,
    project_weight_average,
    query_bias_average,
    value_bias_average,
    output_weight_average,
    output_bias_average,
    first_gain_average,
    first_shift_average,
    up_weight_average,
    up_bias_average,
    down_weight_average,
    down_bias_average,
    second_gain_average,
    second_shift_average,
    sequence_table_average,
    horizontal_table_average,
    vertical_table_average,
):
    total_rows, model_width = tokens.shape
    local_width = project_weight.shape[2]
    local_heads = sequence_table.shape[1]
    hidden = up_weight.shape[1]
    share_rows = total_rows // lax.axis_size("head")
    head_index = lax.axis_index("head")
    share_start = head_index * share_rows
    block_rows = 128
    off = jnp.full((1,), head_index * (share_rows // block_rows), I32)
    buckets = (sequence_bucket, horizontal_bucket, vertical_bucket)
    tables = (sequence_table, horizontal_table, vertical_table)
    bits = tuple((t.shape[0] - 1).bit_length() for t in tables)
    flat_project = project_weight.reshape(model_width, 3 * local_width)

    small = jnp.concatenate(
        [query_bias, value_bias, up_bias] + [t.reshape(-1) for t in tables]
    ).reshape(1, -1)
    project_weights = (flat_project, fetch_other(flat_project))
    small_other = swap_head(small)[0]
    output_weights = (output_weight, fetch_other(output_weight))
    up_weights = (up_weight, fetch_other(up_weight))
    down_weights = (down_weight, fetch_other(down_weight))
    cuts = [local_width, 2 * local_width, 2 * local_width + hidden]
    ends = []
    for t in tables:
        ends.append(cuts[-1] + t.size)
        cuts.append(ends[-1])
    other_query_bias = small_other[: cuts[0]]
    other_value_bias = small_other[cuts[0] : cuts[1]]
    other_up_bias = small_other[cuts[1] : cuts[2]]
    other_tables = tuple(
        small_other[cuts[2 + i] : cuts[3 + i]].reshape(t.shape) for i, t in enumerate(tables)
    )
    query_biases = (query_bias, other_query_bias)
    value_biases = (value_bias, other_value_bias)
    up_biases = (up_bias, other_up_bias)
    packed_tables = (pack_tables(tables), pack_tables(other_tables))

    form_row = form_number.reshape(1, total_rows)
    form_column = form_number.reshape(total_rows, 1)
    own_tokens = rows_of(tokens, head_index, share_rows)

    scaled, keys, values_t, probs, contexts = [], [], [], [], []
    attend = output_bias.astype(F32)
    for s in range(2):
        wq = project_weights[s][:, :local_width]
        wk = project_weights[s][:, local_width : 2 * local_width]
        wv = project_weights[s][:, 2 * local_width :]
        bv = value_biases[s].astype(F32)
        q = ((mm(own_tokens, wq) + query_biases[s].astype(F32)) * 0.125).astype(BF16)
        q = q * jnp.array(2.0**SCALE_BITS, BF16)
        k = mm(tokens, wk).astype(BF16)
        kt = dot_general_t(wk, tokens).astype(BF16)
        v = (mm(tokens, wv) + bv).astype(BF16)
        vt = (dot_general_t(wv, tokens) + bv[:, None]).astype(BF16)
        p, context = attend_fwd(
            off, buckets, form_column, form_row, packed_tables[s], q, kt, v, qb=block_rows
        )
        attend = attend + mm(context, output_weights[s])
        scaled.append(q)
        keys.append(k)
        values_t.append(vt)
        probs.append(p)
        contexts.append(context)
    n1, root1 = normalize(own_tokens.astype(F32) + attend)
    normed = n1 * first_gain.astype(F32) + first_shift.astype(F32)
    normed_low = normed.astype(BF16)
    feed = down_bias.astype(F32)
    acts, slopes = [], []
    for s in range(2):
        up = mm(normed_low, up_weights[s]) + up_biases[s].astype(F32)
        act, slope = gelu_parts(up)
        act = act.astype(BF16)
        feed = feed + mm(act, down_weights[s])
        acts.append(act)
        slopes.append(slope.astype(BF16))
    n2, root2 = normalize(normed + feed)
    layer_output = n2 * second_gain.astype(F32) + second_shift.astype(F32)

    cot = cotangent.astype(F32)
    back_second = normalize_back(cot * second_gain.astype(F32), n2, root2)
    second_gain_part = jnp.sum(cot * n2, axis=0)
    second_shift_part = jnp.sum(cot, axis=0)
    back_feed = back_second.astype(BF16)
    down_bias_part = jnp.sum(back_feed.astype(F32), axis=0)
    back_normed = back_second
    up_bias_parts, down_grads, up_grads = [], [], []
    for s in range(2):
        down_grads.append(dot_tn(acts[s], back_feed).astype(BF16))
        back_up = (dot_nt(back_feed, down_weights[s]) * slopes[s].astype(F32)).astype(BF16)
        up_bias_parts.append(jnp.sum(back_up.astype(F32), axis=0))
        up_grads.append(dot_tn(normed_low, back_up).astype(BF16))
        back_normed = back_normed + dot_nt(back_up, up_weights[s])
    down_total = reduce_grad(down_grads[0], down_grads[1], True)
    up_total = reduce_grad(up_grads[0], up_grads[1], False)
    first_gain_part = jnp.sum(back_normed * n1, axis=0)
    first_shift_part = jnp.sum(back_normed, axis=0)
    back_first = normalize_back(back_normed * first_gain.astype(F32), n1, root1)
    back_attend = back_first.astype(BF16)
    output_bias_part = jnp.sum(back_attend.astype(F32), axis=0)
    output_grads = [dot_tn(contexts[s], back_attend).astype(BF16) for s in range(2)]
    output_total = reduce_grad(output_grads[0], output_grads[1], True)

    tokens_part = back_first
    other_part = jnp.zeros((share_rows, model_width), F32)
    back_scores, project_grads, query_bias_parts, value_bias_parts = [], [], [], []
    for s in range(2):
        wq = project_weights[s][:, :local_width]
        wk = project_weights[s][:, local_width : 2 * local_width]
        wv = project_weights[s][:, 2 * local_width :]
        back_context = dot_nt(back_attend, output_weights[s]).astype(BF16)
        ds, dq, dkt, dvt = attend_bwd(
            scaled[s], keys[s], values_t[s], back_context, probs[s], qb=block_rows
        )
        dkt = (dkt * 2.0**-SCALE_BITS).astype(BF16)
        dvt = dvt.astype(BF16)
        back_scores.append(ds)
        query_bias_parts.append(jnp.sum(dq.astype(F32), axis=0))
        value_bias_parts.append(jnp.sum(dvt.astype(F32), axis=1))
        project_grads.append(
            jnp.concatenate(
                [dot_tn(own_tokens, dq), dot_tt(tokens, dkt), dot_tt(tokens, dvt)], axis=1
            ).astype(BF16)
        )
        tokens_part = tokens_part + dot_nt(dq, wq)
        for grad, weight in ((dkt, wk), (dvt, wv)):
            own = lax.dynamic_slice_in_dim(grad, share_start, share_rows, 1)
            far = lax.dynamic_slice_in_dim(grad, (1 - head_index) * share_rows, share_rows, 1)
            tokens_part = tokens_part + dot_tt(own, weight)
            other_part = other_part + dot_tt(far, weight)
    tokens_gradient = tokens_part + swap_head(other_part.astype(BF16)).astype(F32)
    project_total = reduce_grad(project_grads[0], project_grads[1], True).reshape(
        model_width, 3, local_width
    )
    counts = hist(off, buckets, back_scores[0], back_scores[1], bits, qb=block_rows)
    table_parts = [unhist(a, b, 2 * local_heads) for a, b in zip(counts, bits)]

    common = [
        first_gain_part,
        first_shift_part,
        second_gain_part,
        second_shift_part,
        output_bias_part,
        down_bias_part,
    ]
    halves = [
        [query_bias_parts[s], value_bias_parts[s], up_bias_parts[s]]
        + [t[:, s * local_heads : (s + 1) * local_heads].reshape(-1) for t in table_parts]
        for s in range(2)
    ]
    sizes = [a.size for a in common + halves[0]]
    padding = -sum(sizes) % 1024
    mine = jnp.concatenate(common + halves[0] + [jnp.zeros((padding,), F32)]).reshape(-1, 128)
    theirs = jnp.concatenate(common + halves[1] + [jnp.zeros((padding,), F32)]).reshape(-1, 128)
    sums = mine + swap_head(theirs)
    for bit in dp_bits():
        sums = sums + swap_dp(sums, bit)
    sums = sums.reshape(-1)
    totals, at = [], 0
    for size in sizes:
        totals.append(sums[at : at + size])
        at += size
    (
        first_gain_total,
        first_shift_total,
        second_gain_total,
        second_shift_total,
        output_bias_total,
        down_bias_total,
        query_bias_total,
        value_bias_total,
        up_bias_total,
        sequence_total,
        horizontal_total,
        vertical_total,
    ) = totals
    sequence_total = sequence_total.reshape(sequence_table.shape)
    horizontal_total = horizontal_total.reshape(horizontal_table.shape)
    vertical_total = vertical_total.reshape(vertical_table.shape)
    up_weight_total, down_weight_total, output_weight_total = up_total, down_total, output_total
    token_count = total_rows * lax.axis_size("dp")
    group_count = lax.axis_size("dp")
    group_index = lax.axis_index("dp")

    def renew(average, weight, gradient):
        return 0.5 * average + 0.5 * (weight.astype(jnp.float32) - gradient / token_count)

    def part_of(array, along):
        width = array.shape[along] // group_count
        return lax.dynamic_slice_in_dim(array, group_index * width, width, along)

    return (
        layer_output,
        tokens_gradient,
        project_total,
        query_bias_total,
        value_bias_total,
        output_weight_total,
        output_bias_total,
        first_gain_total,
        first_shift_total,
        up_weight_total,
        up_bias_total,
        down_weight_total,
        down_bias_total,
        second_gain_total,
        second_shift_total,
        sequence_total,
        horizontal_total,
        vertical_total,
        renew(project_weight_average, part_of(project_weight, 0), part_of(project_total, 0)),
        renew(query_bias_average, query_bias, query_bias_total),
        renew(value_bias_average, value_bias, value_bias_total),
        renew(output_weight_average, part_of(output_weight, 1), part_of(output_weight_total, 1)),
        renew(output_bias_average, output_bias, output_bias_total),
        renew(first_gain_average, first_gain, first_gain_total),
        renew(first_shift_average, first_shift, first_shift_total),
        renew(up_weight_average, part_of(up_weight, 0), part_of(up_weight_total, 0)),
        renew(up_bias_average, up_bias, up_bias_total),
        renew(down_weight_average, part_of(down_weight, 0), part_of(down_weight_total, 0)),
        renew(down_bias_average, down_bias, down_bias_total),
        renew(second_gain_average, second_gain, second_gain_total),
        renew(second_shift_average, second_shift, second_shift_total),
        renew(sequence_table_average, sequence_table, sequence_total),
        renew(horizontal_table_average, horizontal_table, horizontal_total),
        renew(vertical_table_average, vertical_table, vertical_total),
    )


def solution(mesh):
    in_specs = (
        P("dp", None),
        P(("dp", "head"), None),
        P("dp", None),
        P("dp", None),
        P("dp", None),
        P("dp", None),
        P(None, None, "head"),
        P("head"),
        P("head"),
        P("head", None),
        P(),
        P(),
        P(),
        P(None, "head"),
        P("head"),
        P("head", None),
        P(),
        P(),
        P(),
        P(None, "head"),
        P(None, "head"),
        P(None, "head"),
        P("dp", None, "head"),
        P("head"),
        P("head"),
        P("head", "dp"),
        P(),
        P(),
        P(),
        P("dp", "head"),
        P("head"),
        P(("head", "dp"), None),
        P(),
        P(),
        P(),
        P(None, "head"),
        P(None, "head"),
        P(None, "head"),
    )
    out_specs = (
        P(("dp", "head"), None),
        P(("dp", "head"), None),
        P(None, None, "head"),
        P("head"),
        P("head"),
        P("head", None),
        P(),
        P(),
        P(),
        P(None, "head"),
        P("head"),
        P("head", None),
        P(),
        P(),
        P(),
        P(None, "head"),
        P(None, "head"),
        P(None, "head"),
        P("dp", None, "head"),
        P("head"),
        P("head"),
        P("head", "dp"),
        P(),
        P(),
        P(),
        P("dp", "head"),
        P("head"),
        P(("head", "dp"), None),
        P(),
        P(),
        P(),
        P(None, "head"),
        P(None, "head"),
        P(None, "head"),
    )
    return jax.shard_map(local, mesh=mesh, in_specs=in_specs, out_specs=out_specs, check_vma=False)
```

time: 1120 us -> 589 us (0.53)
  matrix products: 427 us -> 81.3 us
  waiting for transfers between devices: 293 us -> 163 us
  Pallas kernels: 0 us -> 114 us
  local copies, waits for them, and re-layouts: 189 us -> 79.6 us
  blocking collectives: 102 us -> 0 us
  starting transfers between devices: 0.58 us -> 51.5 us
  between operations: 15.6 us -> 3.07 us
    dot_general x36 -> x45, matrix products: 427 us -> 81.3 us  [the longest x11 26.1 us: mm(): return jnp.dot(a, b, preferred_element_type=F32)]
    ppermute x0 -> x60, waiting for transfers between devices: none -> 163 us  [the longest x49 130 us: swap_dp(): return lax.ppermute(x, 'dp', [(i, i ^ bit) for i in range(n)])]
    reduce_scatter x4 -> x0, waiting for transfers between devices: 129 us -> none  [the longest x1 46.1 us: local(): lax.psum_scatter(jnp.dot(picked, output_weight, preferred_element_type=jn...]
    pallas_call x0 -> x5, Pallas kernels: none -> 114 us  [the longest x2 54.1 us: attend_fwd(): pl.pallas_call(functools.partial(fwd_kernel, pairs=pairs, qb=qb), out_sha...]
    psum x2 -> x0, blocking collectives: 102 us -> none  [the longest x1 62 us: local(): lax.psum((up_weight_gradient, up_bias_gradient, down_weight_gradient, dow...]
    dot_general x6 -> x2, local copies, waits for them, and re-layouts: 94.4 us -> 0.19 us  [unhist(): jnp.einsum('fhv,fb,vb->bh', m, lhs, var, precision=lax.Precision.HIGHEST)]
    psum x1 -> x0, waiting for transfers between devices: 90.3 us -> none  [local(): lax.psum((up_weight_gradient, up_bias_gradient, down_weight_gradient, dow...]
    all_gather x3 -> x0, waiting for transfers between devices: 73.6 us -> none  [the longest x1 27.3 us: local(): lax.all_gather(normed.astype(jnp.bfloat16), 'head', axis=0, tiled=True)]
  transfers between devices with their start and end apart: 8 -> 60, of which waited for: 7 -> 25; matrix products, arithmetic and copies ran while one was open for 17% -> 29% of each run, Pallas kernels for 0% -> 15%
where the time goes in v1:
time: 589 us; the launch traced here: 581 us
  waiting for transfers between devices  163 us (28%)
  Pallas kernels  114 us (19%)
  other arithmetic  88.1 us (15%)
  matrix products  81.3 us (14%)
  local copies, waits for them, and re-layouts  79.6 us (14%)
  starting transfers between devices  51.5 us (9%)
    ppermute x49, waiting for transfers between devices, swap_dp(): return lax.ppermute(x, 'dp', [(i, i ^ bit) for i in range(n)])  130 us
    pallas_call x2, Pallas kernels, attend_fwd(): pl.pallas_call(functools.partial(fwd_kernel, pairs=pairs, qb=qb), out_sha...  54.1 us
    ppermute x49, starting transfers between devices, swap_dp(): return lax.ppermute(x, 'dp', [(i, i ^ bit) for i in range(n)])  39.8 us
    pallas_call x1, Pallas kernels, hist(): pl.pallas_call(functools.partial(hist_kernel, qb=qb, bits=bits), out_shap...  34.3 us
    ppermute x11, waiting for transfers between devices, swap_head(): return lax.ppermute(x, 'head', [(0, 1), (1, 0)])  32.4 us
    unnamed x290, local copies, waits for them, and re-layouts  26.3 us
    pallas_call x2, Pallas kernels, attend_bwd(): pl.pallas_call(functools.partial(bwd_kernel, pairs=pairs, qb=qb), out_sha...  26.1 us
    dot_general x11, matrix products, mm(): return jnp.dot(a, b, preferred_element_type=F32)  26.1 us
  transfers between devices with their start and end apart: 60, of which 25 were waited for; matrix products, arithmetic and copies ran while one was open for 29% of the time, Pallas kernels for 15%

profile of v1, /device:TPU:0, one launch (start us, length us, event | category | flops | bytes accessed | tf_op | source)
XLA Modules:
  0.0 580.8 jit_solution(6162495053066314332)
XLA Ops:
  6.2 3.0 collective-permute-start
  40.5 27.2 %shard_map.621 = (bf16[6,512,1024]{2,1,0:T(8,128)(2,1)}, bf16[512,384]{1,0:T(8,128)(2,1)}) custom-call(s32[1]{0:T(128)} %bitcast.4.off, s32[1024,1024]{1,0:T(8,128)} %seq.5, s32[1024,1024]{1,0:T(8,128)} %hor.5, s32[1024,1024]{1,0:T(8,128)} %ver.5, s32[1024,1]{1,0:T(8,128)} %copy.179.formc, s32[1,1024]{1,0:T(1,128)} %formr.3, s32[9,128]{1,0:T(8,128)} %add.588.tab, ...), custom_call_target="tpu_custom_call" | custom-call | flops 805306368 | bytes 16777216 | tf_op jit(solution)/shard_map/pallas_call | solution.py:86
  97.7 4.0 collective-permute-done.2
  103.5 10.9 %collective-permute-done.8 = bf16[192,1536]{1,0:T(8,128)(2,1)} collective-permute-done((bf16[192,1536]{1,0:T(8,128)(2,1)}, bf16[192,1536]{1,0:T(8,128)(2,1)}, u32[]{:S(2)}, u32[]{:S(2)}) %collective-permute-start.8) | collective-permute-done | bytes 589856 | tf_op jit(solution)/shard_map/ppermute | solution.py:285
  117.1 9.3 %collective-permute-done.11 = bf16[384,768]{1,0:T(8,128)(2,1)S(1)} collective-permute-done((bf16[384,768]{1,0:T(8,128)(2,1)}, bf16[384,768]{1,0:T(8,128)(2,1)S(1)}, u32[]{:S(2)}, u32[]{:S(2)}) %collective-permute-start.11) | collective-permute-done | bytes 589856 | tf_op jit(solution)/shard_map/ppermute | solution.py:285
  136.6 3.3 add_convert_fusion.12.vt
  142.2 26.9 %shard_map.622 = (bf16[6,512,1024]{2,1,0:T(8,128)(2,1)}, bf16[512,384]{1,0:T(8,128)(2,1)}) custom-call(s32[1]{0:T(128)} %bitcast.4.off, s32[1024,1024]{1,0:T(8,128)} %seq.5, s32[1024,1024]{1,0:T(8,128)} %hor.5, s32[1024,1024]{1,0:T(8,128)} %ver.5, s32[1024,1]{1,0:T(8,128)} %copy.179.formc, s32[1,1024]{1,0:T(1,128)} %formr.3, s32[9,128]{1,0:T(8,128)} %add.595.tab, ...), custom_call_target="tpu_custom_call" | custom-call | flops 805306368 | bytes 16777216 | tf_op jit(solution)/shard_map/pallas_call | solution.py:86
  172.8 3.6 multiply_convert_fusion.1
  180.0 4.4 multiply_convert_fusion
  193.4 6.0 %convert_reduce_fusion = (f32[1536]{0:T(1024)}, bf16[512,1536]{1,0:T(8,128)(2,1)S(1)}) fusion(f32[512,1536]{1,0:T(8,128)S(1)} %get-tuple-element.341, bf16[512,768]{1,0:T(8,128)(2,1)S(1)} %get-tuple-element.246, bf16[768,768]{1,0:T(8,128)(2,1)S(1)} %get-tuple-element.255, bf16[768,768]{1,0:T(8,128)(2,1)S(1)} %get-tuple-element.254), kind=kOutput, calls=%fused_computation.14 | convolution fusion | flops 1235483136 | bytes 7870464 | tf_op jit(solution)/shard_map/dot_general | solution.py:16
  199.4 4.2 convert_reduce_fusion.1
  212.8 12.8 %shard_map.624 = (bf16[6,512,1024]{2,1,0:T(8,128)(2,1)}, bf16[512,384]{1,0:T(8,128)(2,1)}, f32[384,1024]{1,0:T(8,128)}, f32[384,1024]{1,0:T(8,128)}) custom-call(bf16[512,384]{1,0:T(8,128)(2,1)} %fusion.22.q, bf16[1024,384]{1,0:T(8,128)(2,1)} %bitcast.161, bf16[384,1024]{1,0:T(8,128)(2,1)} %add_convert_fusion.12.vt, ...), custom_call_target="tpu_custom_call" | custom-call | flops 1610612736 | bytes 31457280 | tf_op jit(solution)/shard_map/pallas_call | solution.py:154
  229.6 13.3 %shard_map.623 = (bf16[6,512,1024]{2,1,0:T(8,128)(2,1)}, bf16[512,384]{1,0:T(8,128)(2,1)}, f32[384,1024]{1,0:T(8,128)}, f32[384,1024]{1,0:T(8,128)}) custom-call(bf16[512,384]{1,0:T(8,128)(2,1)} %fusion.23.q, bf16[1024,384]{1,0:T(8,128)(2,1)} %convolution_convert_fusion.4.k, bf16[384,1024]{1,0:T(8,128)(2,1)} %add_convert_fusion.11.vt, ...), custom_call_target="tpu_custom_call" | custom-call | flops 1610612736 | bytes 31457280 | tf_op jit(solution)/shard_map/pallas_call | solution.py:154
  273.3 3.0 convolution_convert_fusion.1
  281.5 34.3 %shard_map.625 = (f32[128,192]{1,0:T(8,128)}, f32[256,192]{1,0:T(8,128)}, f32[256,192]{1,0:T(8,128)}) custom-call(s32[1]{0:T(128)} %bitcast.4.off, s32[1024,1024]{1,0:T(8,128)} %seq.5, s32[1024,1024]{1,0:T(8,128)} %hor.5, s32[1024,1024]{1,0:T(8,128)} %ver.5, bf16[6,512,1024]{2,1,0:T(8,128)(2,1)} %get-tuple-element.59.dsa, ...), custom_call_target="tpu_custom_call" | custom-call | flops 16106127360 | bytes 20971520 | tf_op jit(solution)/shard_map/pallas_call | solution.py:211
  321.3 3.4 reshape.387
  352.7 7.4 %collective-permute-done.31 = bf16[192,768]{1,0:T(8,128)(2,1)} collective-permute-done((bf16[192,768]{1,0:T(8,128)(2,1)S(1)}, bf16[192,768]{1,0:T(8,128)(2,1)}, u32[]{:S(2)}, u32[]{:S(2)}) %collective-permute-start.31) | collective-permute-done | bytes 294944 | tf_op jit(solution)/shard_map/ppermute | solution.py:289
  389.3 5.5 convert_add_fusion
  398.2 3.1 collective-permute-done.37
  416.0 7.9 %collective-permute-done.16 = bf16[384,1152]{0,1:T(8,128)(2,1)S(1)} collective-permute-done((bf16[384,1152]{0,1:T(8,128)(2,1)S(1)}, bf16[384,1152]{0,1:T(8,128)(2,1)S(1)}, u32[]{:S(2)}, u32[]{:S(2)}) %collective-permute-start.16) | collective-permute-done | bytes 884768 | tf_op jit(solution)/shard_map/ppermute | solution.py:289
  430.1 13.3 %collective-permute-done.17 = bf16[192,1152]{1,0:T(8,128)(2,1)S(1)} collective-permute-done((bf16[192,1152]{1,0:T(8,128)(2,1)S(1)}, bf16[192,1152]{1,0:T(8,128)(2,1)S(1)}, u32[]{:S(2)}, u32[]{:S(2)}) %collective-permute-start.17) | collective-permute-done | bytes 442400 | tf_op jit(solution)/shard_map/ppermute | solution.py:285
  444.5 17.0 %collective-permute-done.43 = bf16[192,1536]{1,0:T(8,128)(2,1)} collective-permute-done((bf16[192,1536]{1,0:T(8,128)(2,1)}, bf16[192,1536]{1,0:T(8,128)(2,1)}, u32[]{:S(2)}, u32[]{:S(2)}) %collective-permute-start.43) | collective-permute-done | bytes 589856 | tf_op jit(solution)/shard_map/ppermute | solution.py:289
  467.3 14.3 %collective-permute-done.19 = bf16[48,1152]{0,1:T(8,128)(2,1)S(1)} collective-permute-done((bf16[48,1152]{0,1:T(8,128)(2,1)S(1)}, bf16[48,1152]{0,1:T(8,128)(2,1)S(1)}, u32[]{:S(2)}, u32[]{:S(2)}) %collective-permute-start.19) | collective-permute-done | bytes 110624 | tf_op jit(solution)/shard_map/ppermute | solution.py:285
  482.0 3.0 collective-permute-start.45
  484.9 13.9 %collective-permute-done.20 = bf16[48,1152]{0,1:T(8,128)(2,1)S(1)} collective-permute-done((bf16[48,1152]{0,1:T(8,128)(2,1)S(1)}, bf16[48,1152]{0,1:T(8,128)(2,1)S(1)}, u32[]{:S(2)}, u32[]{:S(2)}) %collective-permute-start.20) | collective-permute-done | bytes 110624 | tf_op jit(solution)/shard_map/ppermute | solution.py:285
  502.9 7.8 %collective-permute-done.21 = bf16[96,1152]{0,1:T(8,128)(2,1)S(1)} collective-permute-done((bf16[96,1152]{0,1:T(8,128)(2,1)S(1)}, bf16[96,1152]{0,1:T(8,128)(2,1)S(1)}, u32[]{:S(2)}, u32[]{:S(2)}) %collective-permute-start.21) | collective-permute-done | bytes 221216 | tf_op jit(solution)/shard_map/ppermute | solution.py:285
  517.0 7.7 %collective-permute-done.47 = bf16[96,1536]{1,0:T(8,128)(2,1)S(1)} collective-permute-done((bf16[96,1536]{1,0:T(8,128)(2,1)S(1)}, bf16[96,1536]{1,0:T(8,128)(2,1)S(1)}, u32[]{:S(2)}, u32[]{:S(2)}) %collective-permute-start.47) | collective-permute-done | bytes 294944 | tf_op jit(solution)/shard_map/ppermute | solution.py:285
  525.6 3.5 collective-permute-done.54
  531.5 5.8 %collective-permute-done.55 = bf16[96,768]{1,0:T(8,128)(2,1)S(1)} collective-permute-done((bf16[96,768]{1,0:T(8,128)(2,1)S(1)}, bf16[96,768]{1,0:T(8,128)(2,1)S(1)}, u32[]{:S(2)}, u32[]{:S(2)}) %collective-permute-start.55) | collective-permute-done | bytes 147488 | tf_op jit(solution)/shard_map/ppermute | solution.py:285
  537.8 7.9 %collective-permute-done.56 = bf16[96,768]{1,0:T(8,128)(2,1)S(1)} collective-permute-done((bf16[96,768]{1,0:T(8,128)(2,1)S(1)}, bf16[96,768]{1,0:T(8,128)(2,1)S(1)}, u32[]{:S(2)}, u32[]{:S(2)}) %collective-permute-start.56) | collective-permute-done | bytes 147488 | tf_op jit(solution)/shard_map/ppermute | solution.py:285
  547.2 7.6 %collective-permute-done.57 = bf16[192,768]{1,0:T(8,128)(2,1)S(1)} collective-permute-done((bf16[192,768]{1,0:T(8,128)(2,1)S(1)}, bf16[192,768]{1,0:T(8,128)(2,1)S(1)}, u32[]{:S(2)}, u32[]{:S(2)}) %collective-permute-start.57) | collective-permute-done | bytes 294944 | tf_op jit(solution)/shard_map/ppermute | solution.py:285
  563.9 6.6 %collective-permute-done.58 = bf16[384,768]{1,0:T(8,128)(2,1)} collective-permute-done((bf16[384,768]{1,0:T(8,128)(2,1)}, bf16[384,768]{1,0:T(8,128)(2,1)}, u32[]{:S(2)}, u32[]{:S(2)}) %collective-permute-start.58) | collective-permute-done | bytes 589856 | tf_op jit(solution)/shard_map/ppermute | solution.py:285
  (660 shorter events, 275.7 us)
Async XLA Ops:
  6.2 74.2 %collective-permute-start = (bf16[1,3264]{1,0:T(2,128)(2,1)}, bf16[1,3264]{1,0:T(2,128)(2,1)}, u32[]{:S(2)}, u32[]{:S(2)}) collective-permute-start(bf16[1,3264]{1,0:T(2,128)(2,1)} %reshape.384), channel_id=1, source_target_pairs={{0,1},{1,0},{2,3},{3,2},{4,5},{5,4},{6,7},{7,6},{8,9},{9,8},{10,11... | collective-permute-start | bytes 19592 | tf_op jit(solution)/shard_map/ppermute | solution.py:289
  13.1 75.3 %collective-permute-start.1 = (bf16[192,1152]{1,0:T(8,128)(2,1)}, bf16[192,1152]{1,0:T(8,128)(2,1)}, u32[]{:S(2)}, u32[]{:S(2)}) collective-permute-start(bf16[192,1152]{1,0:T(8,128)(2,1)} %copy.187), channel_id=1, source_target_pairs={{0,1},{1,0},{2,3},{3,2},{4,5},{5,4},{6,7},{7,6},{8,9},{9,8},{10,11... | collective-permute-start | bytes 1327112 | tf_op jit(solution)/shard_map/ppermute | solution.py:289
  14.2 67.1 %collective-permute-start.4 = (bf16[96,768]{1,0:T(8,128)(2,1)S(1)}, bf16[96,768]{1,0:T(8,128)(2,1)}, u32[]{:S(2)}, u32[]{:S(2)}) collective-permute-start(bf16[96,768]{1,0:T(8,128)(2,1)S(1)} %constant_dynamic-slice_fusion.23), channel_id=1, source_target_pairs={{0,1},{1,0},{2,3},{3,2},{4,5},{5,4},{6,7},{7,6},{8,9},{9,8},{10,11... | collective-permute-start | bytes 442376 | tf_op jit(solution)/shard_map/ppermute | solution.py:289
  18.0 75.7 %collective-permute-start.7 = (bf16[192,1536]{1,0:T(8,128)(2,1)}, bf16[192,1536]{1,0:T(8,128)(2,1)}, u32[]{:S(2)}, u32[]{:S(2)}) collective-permute-start(bf16[192,1536]{1,0:T(8,128)(2,1)} %constant_dynamic-slice_fusion.22), channel_id=1, source_target_pairs={{0,1},{1,0},{2,3},{3,2},{4,5},{5,4},{6,7},{7,6},{8,9},{9,8},{10,11... | collective-permute-start | bytes 1769480 | tf_op jit(solution)/shard_map/ppermute | solution.py:289
  20.1 74.3 %collective-permute-start.10 = (bf16[384,768]{1,0:T(8,128)(2,1)}, bf16[384,768]{1,0:T(8,128)(2,1)}, u32[]{:S(2)}, u32[]{:S(2)}) collective-permute-start(bf16[384,768]{1,0:T(8,128)(2,1)} %constant_dynamic-slice_fusion.21), channel_id=1, source_target_pairs={{0,1},{1,0},{2,3},{3,2},{4,5},{5,4},{6,7},{7,6},{8,9},{9,8},{10,11... | collective-permute-start | bytes 1769480 | tf_op jit(solution)/shard_map/ppermute | solution.py:289
  93.8 20.6 %collective-permute-start.8 = (bf16[192,1536]{1,0:T(8,128)(2,1)}, bf16[192,1536]{1,0:T(8,128)(2,1)}, u32[]{:S(2)}, u32[]{:S(2)}) collective-permute-start(bf16[192,1536]{1,0:T(8,128)(2,1)} %collective-permute-done.7), channel_id=1, source_target_pairs={{0,4},{2,6},{4,0},{6,2},{8,12},{10,14},{12,8},{14,10},{16,20},{18,... | collective-permute-start | bytes 1769480 | tf_op jit(solution)/shard_map/ppermute | solution.py:285
  94.4 32.1 %collective-permute-start.11 = (bf16[384,768]{1,0:T(8,128)(2,1)}, bf16[384,768]{1,0:T(8,128)(2,1)S(1)}, u32[]{:S(2)}, u32[]{:S(2)}) collective-permute-start(bf16[384,768]{1,0:T(8,128)(2,1)} %collective-permute-done.10), channel_id=1, source_target_pairs={{0,4},{2,6},{4,0},{6,2},{8,12},{10,14},{12,8},{14,10},{16,20},{18,... | collective-permute-start | bytes 1769480 | tf_op jit(solution)/shard_map/ppermute | solution.py:285
  103.4 25.6 %collective-permute-start.3 = (bf16[384,1152]{0,1:T(8,128)(2,1)S(1)}, bf16[384,1152]{0,1:T(8,128)(2,1)S(1)}, u32[]{:S(2)}, u32[]{:S(2)}) collective-permute-start(bf16[384,1152]{0,1:T(8,128)(2,1)S(1)} %pad_maximum_fusion.16), channel_id=1, source_target_pairs={{0,2},{2,0},{4,6},{6,4},{8,10},{10,8},{12,14},{14,12},{16,18},{18,... | collective-permute-start | bytes 2654216 | tf_op jit(solution)/shard_map/ppermute | solution.py:285
  116.9 61.0 %collective-permute-start.9 = (bf16[384,1536]{1,0:T(8,128)(2,1)}, bf16[384,1536]{1,0:T(8,128)(2,1)}, u32[]{:S(2)}, u32[]{:S(2)}) collective-permute-start(bf16[384,1536]{1,0:T(8,128)(2,1)} %pad_maximum_fusion.12), channel_id=1, source_target_pairs={{0,2},{2,0},{4,6},{6,4},{8,10},{10,8},{12,14},{14,12},{16,18},{18,... | collective-permute-start | bytes 3538952 | tf_op jit(solution)/shard_map/ppermute | solution.py:285
  128.8 55.7 %collective-permute-start.12 = (bf16[768,768]{1,0:T(8,128)(2,1)}, bf16[768,768]{1,0:T(8,128)(2,1)}, u32[]{:S(2)}, u32[]{:S(2)}) collective-permute-start(bf16[768,768]{1,0:T(8,128)(2,1)} %pad_maximum_fusion.13), channel_id=1, source_target_pairs={{0,2},{2,0},{4,6},{6,4},{8,10},{10,8},{12,14},{14,12},{16,18},{18,... | collective-permute-start | bytes 3538952 | tf_op jit(solution)/shard_map/ppermute | solution.py:285
  277.9 108.9 %collective-permute-start.13 = (bf16[512,768]{1,0:T(8,128)(2,1)}, bf16[512,768]{1,0:T(8,128)(2,1)}, u32[]{:S(2)}, u32[]{:S(2)}) collective-permute-start(bf16[512,768]{1,0:T(8,128)(2,1)} %add_convert_fusion.10), channel_id=1, source_target_pairs={{0,1},{1,0},{2,3},{3,2},{4,5},{5,4},{6,7},{7,6},{8,9},{9,8},{10,11... | collective-permute-start | bytes 2359304 | tf_op jit(solution)/shard_map/ppermute | solution.py:289
  279.4 115.8 %collective-permute-start.15 = (bf16[384,1152]{0,1:T(8,128)(2,1)}, bf16[384,1152]{0,1:T(8,128)(2,1)}, u32[]{:S(2)}, u32[]{:S(2)}) collective-permute-start(bf16[384,1152]{0,1:T(8,128)(2,1)} %constant_dynamic-slice_fusion.19), channel_id=1, source_target_pairs={{0,2},{2,0},{4,6},{6,4},{8,10},{10,8},{12,14},{14,12},{16,18},{18,... | collective-permute-start | bytes 2654216 | tf_op jit(solution)/shard_map/ppermute | solution.py:285
  281.2 133.4 %collective-permute-start.14 = (bf16[384,1152]{0,1:T(8,128)(2,1)}, bf16[384,1152]{0,1:T(8,128)(2,1)}, u32[]{:S(2)}, u32[]{:S(2)}) collective-permute-start(bf16[384,1152]{0,1:T(8,128)(2,1)} %constant_dynamic-slice_fusion.20), channel_id=1, source_target_pairs={{0,2},{2,0},{4,6},{6,4},{8,10},{10,8},{12,14},{14,12},{16,18},{18,... | collective-permute-start | bytes 2654216 | tf_op jit(solution)/shard_map/ppermute | solution.py:285
  352.4 49.0 %collective-permute-start.41 = (bf16[384,1536]{1,0:T(8,128)(2,1)}, bf16[384,1536]{1,0:T(8,128)(2,1)}, u32[]{:S(2)}, u32[]{:S(2)}) collective-permute-start(bf16[384,1536]{1,0:T(8,128)(2,1)} %constant_dynamic-slice_fusion.8), channel_id=1, source_target_pairs={{0,2},{2,0},{4,6},{6,4},{8,10},{10,8},{12,14},{14,12},{16,18},{18,... | collective-permute-start | bytes 3538952 | tf_op jit(solution)/shard_map/ppermute | solution.py:285
  386.7 17.9 %collective-permute-start.39 = (bf16[384,1536]{1,0:T(8,128)(2,1)}, bf16[384,1536]{1,0:T(8,128)(2,1)S(1)}, u32[]{:S(2)}, u32[]{:S(2)}) collective-permute-start(bf16[384,1536]{1,0:T(8,128)(2,1)} %constant_dynamic-slice_fusion.10), channel_id=1, source_target_pairs={{0,2},{2,0},{4,6},{6,4},{8,10},{10,8},{12,14},{14,12},{16,18},{18,... | collective-permute-start | bytes 3538952 | tf_op jit(solution)/shard_map/ppermute | solution.py:285
  401.3 61.9 %collective-permute-start.50 = (bf16[768,768]{1,0:T(8,128)(2,1)}, bf16[768,768]{1,0:T(8,128)(2,1)}, u32[]{:S(2)}, u32[]{:S(2)}) collective-permute-start(bf16[768,768]{1,0:T(8,128)(2,1)} %constant_dynamic-slice_fusion.4), channel_id=1, source_target_pairs={{0,2},{2,0},{4,6},{6,4},{8,10},{10,8},{12,14},{14,12},{16,18},{18,... | collective-permute-start | bytes 3538952 | tf_op jit(solution)/shard_map/ppermute | solution.py:285
  401.4 22.5 %collective-permute-start.16 = (bf16[384,1152]{0,1:T(8,128)(2,1)S(1)}, bf16[384,1152]{0,1:T(8,128)(2,1)S(1)}, u32[]{:S(2)}, u32[]{:S(2)}) collective-permute-start(bf16[384,1152]{0,1:T(8,128)(2,1)S(1)} %add_convert_fusion.8), channel_id=1, source_target_pairs={{0,1},{1,0},{2,3},{3,2},{4,5},{5,4},{6,7},{7,6},{8,9},{9,8},{10,11... | collective-permute-start | bytes 2654216 | tf_op jit(solution)/shard_map/ppermute | solution.py:289
  405.5 22.0 %collective-permute-start.42 = (bf16[192,1536]{1,0:T(8,128)(2,1)}, bf16[192,1536]{1,0:T(8,128)(2,1)}, u32[]{:S(2)}, u32[]{:S(2)}) collective-permute-start(bf16[192,1536]{1,0:T(8,128)(2,1)} %constant_dynamic-slice_fusion.7), channel_id=1, source_target_pairs={{0,4},{2,6},{4,0},{6,2},{8,12},{10,14},{12,8},{14,10},{16,20},{18,... | collective-permute-start | bytes 1769480 | tf_op jit(solution)/shard_map/ppermute | solution.py:285
  409.3 35.3 %collective-permute-start.40 = (bf16[192,1536]{1,0:T(8,128)(2,1)}, bf16[192,1536]{1,0:T(8,128)(2,1)}, u32[]{:S(2)}, u32[]{:S(2)}) collective-permute-start(bf16[192,1536]{1,0:T(8,128)(2,1)} %constant_dynamic-slice_fusion.9), channel_id=1, source_target_pairs={{0,4},{2,6},{4,0},{6,2},{8,12},{10,14},{12,8},{14,10},{16,20},{18,... | collective-permute-start | bytes 1769480 | tf_op jit(solution)/shard_map/ppermute | solution.py:285
  414.6 48.6 %collective-permute-start.52 = (bf16[768,768]{1,0:T(8,128)(2,1)}, bf16[768,768]{1,0:T(8,128)(2,1)}, u32[]{:S(2)}, u32[]{:S(2)}) collective-permute-start(bf16[768,768]{1,0:T(8,128)(2,1)} %add_convert_fusion.3), channel_id=1, source_target_pairs={{0,1},{1,0},{2,3},{3,2},{4,5},{5,4},{6,7},{7,6},{8,9},{9,8},{10,11... | collective-permute-start | bytes 3538952 | tf_op jit(solution)/shard_map/ppermute | solution.py:289
  426.0 17.4 %collective-permute-start.17 = (bf16[192,1152]{1,0:T(8,128)(2,1)S(1)}, bf16[192,1152]{1,0:T(8,128)(2,1)S(1)}, u32[]{:S(2)}, u32[]{:S(2)}) collective-permute-start(bf16[192,1152]{1,0:T(8,128)(2,1)S(1)} %copy.196), channel_id=1, source_target_pairs={{0,4},{2,6},{4,0},{6,2},{8,12},{10,14},{12,8},{14,10},{16,20},{18,... | collective-permute-start | bytes 1327112 | tf_op jit(solution)/shard_map/ppermute | solution.py:285
  429.6 32.0 %collective-permute-start.43 = (bf16[192,1536]{1,0:T(8,128)(2,1)}, bf16[192,1536]{1,0:T(8,128)(2,1)}, u32[]{:S(2)}, u32[]{:S(2)}) collective-permute-start(bf16[192,1536]{1,0:T(8,128)(2,1)} %add_convert_fusion.16), channel_id=1, source_target_pairs={{0,1},{1,0},{2,3},{3,2},{4,5},{5,4},{6,7},{7,6},{8,9},{9,8},{10,11... | collective-permute-start | bytes 1769480 | tf_op jit(solution)/shard_map/ppermute | solution.py:289
  444.4 20.9 %collective-permute-start.18 = (bf16[96,1152]{0,1:T(8,128)(2,1)S(1)}, bf16[96,1152]{0,1:T(8,128)(2,1)S(1)}, u32[]{:S(2)}, u32[]{:S(2)}) collective-permute-start(bf16[96,1152]{0,1:T(8,128)(2,1)S(1)} %constant_dynamic-slice_fusion.17), channel_id=1, source_target_pairs={{0,8},{2,10},{4,12},{6,14},{8,0},{10,2},{12,4},{14,6},{16,24},{18,... | collective-permute-start | bytes 663560 | tf_op jit(solution)/shard_map/ppermute | solution.py:285
  463.1 18.8 %collective-permute-start.44 = (bf16[96,1536]{1,0:T(8,128)(2,1)S(1)}, bf16[96,1536]{1,0:T(8,128)(2,1)S(1)}, u32[]{:S(2)}, u32[]{:S(2)}) collective-permute-start(bf16[96,1536]{1,0:T(8,128)(2,1)S(1)} %constant_dynamic-slice_fusion.6), channel_id=1, source_target_pairs={{0,8},{2,10},{4,12},{6,14},{8,0},{10,2},{12,4},{14,6},{16,24},{18,... | collective-permute-start | bytes 884744 | tf_op jit(solution)/shard_map/ppermute | solution.py:285
  465.7 15.9 %collective-permute-start.19 = (bf16[48,1152]{0,1:T(8,128)(2,1)S(1)}, bf16[48,1152]{0,1:T(8,128)(2,1)S(1)}, u32[]{:S(2)}, u32[]{:S(2)}) collective-permute-start(bf16[48,1152]{0,1:T(8,128)(2,1)S(1)} %constant_dynamic-slice_fusion.16), channel_id=1, source_target_pairs={{0,16},{2,18},{4,20},{6,22},{8,24},{10,26},{12,28},{14,30},{16,0},... | collective-permute-start | bytes 331784 | tf_op jit(solution)/shard_map/ppermute | solution.py:285
  465.8 49.0 %collective-permute-start.53 = (bf16[384,768]{1,0:T(8,128)(2,1)S(1)}, bf16[384,768]{1,0:T(8,128)(2,1)S(1)}, u32[]{:S(2)}, u32[]{:S(2)}) collective-permute-start(bf16[384,768]{1,0:T(8,128)(2,1)S(1)} %constant_dynamic-slice_fusion.2), channel_id=1, source_target_pairs={{0,4},{2,6},{4,0},{6,2},{8,12},{10,14},{12,8},{14,10},{16,20},{18,... | collective-permute-start | bytes 1769480 | tf_op jit(solution)/shard_map/ppermute | solution.py:285
  481.8 17.1 %collective-permute-start.20 = (bf16[48,1152]{0,1:T(8,128)(2,1)S(1)}, bf16[48,1152]{0,1:T(8,128)(2,1)S(1)}, u32[]{:S(2)}, u32[]{:S(2)}) collective-permute-start(bf16[48,1152]{0,1:T(8,128)(2,1)S(1)} %add_convert_fusion.24), channel_id=1, source_target_pairs={{0,16},{2,18},{4,20},{6,22},{8,24},{10,26},{12,28},{14,30},{16,0},... | collective-permute-start | bytes 331784 | tf_op jit(solution)/shard_map/ppermute | solution.py:285
  482.0 20.0 %collective-permute-start.45 = (bf16[48,1536]{1,0:T(8,128)(2,1)S(1)}, bf16[48,1536]{1,0:T(8,128)(2,1)S(1)}, u32[]{:S(2)}, u32[]{:S(2)}) collective-permute-start(bf16[48,1536]{1,0:T(8,128)(2,1)S(1)} %constant_dynamic-slice_fusion.5), channel_id=1, source_target_pairs={{0,16},{2,18},{4,20},{6,22},{8,24},{10,26},{12,28},{14,30},{16,0},... | collective-permute-start | bytes 442376 | tf_op jit(solution)/shard_map/ppermute | solution.py:285
  512.2 17.7 %collective-permute-start.22 = (bf16[192,1152]{1,0:T(8,128)(2,1)}, bf16[192,1152]{1,0:T(8,128)(2,1)}, u32[]{:S(2)}, u32[]{:S(2)}) collective-permute-start(bf16[192,1152]{1,0:T(8,128)(2,1)} %copy.198), channel_id=1, source_target_pairs={{0,4},{2,6},{4,0},{6,2},{8,12},{10,14},{12,8},{14,10},{16,20},{18,... | collective-permute-start | bytes 1327112 | tf_op jit(solution)/shard_map/ppermute | solution.py:285
  524.8 21.1 %collective-permute-start.48 = (bf16[192,1536]{1,0:T(8,128)(2,1)S(1)}, bf16[192,1536]{1,0:T(8,128)(2,1)S(1)}, u32[]{:S(2)}, u32[]{:S(2)}) collective-permute-start(bf16[192,1536]{1,0:T(8,128)(2,1)S(1)} %pad_maximum_fusion.21), channel_id=1, source_target_pairs={{0,4},{2,6},{4,0},{6,2},{8,12},{10,14},{12,8},{14,10},{16,20},{18,... | collective-permute-start | bytes 1769480 | tf_op jit(solution)/shard_map/ppermute | solution.py:285
  537.8 18.0 %collective-permute-start.23 = (bf16[384,1152]{0,1:T(8,128)(2,1)S(1)}, bf16[384,1152]{0,1:T(8,128)(2,1)S(1)}, u32[]{:S(2)}, u32[]{:S(2)}) collective-permute-start(bf16[384,1152]{0,1:T(8,128)(2,1)S(1)} %pad_maximum_fusion.17), channel_id=1, source_target_pairs={{0,2},{2,0},{4,6},{6,4},{8,10},{10,8},{12,14},{14,12},{16,18},{18,... | collective-permute-start | bytes 2654216 | tf_op jit(solution)/shard_map/ppermute | solution.py:285
  547.2 24.7 %collective-permute-start.49 = (bf16[384,1536]{1,0:T(8,128)(2,1)}, bf16[384,1536]{1,0:T(8,128)(2,1)}, u32[]{:S(2)}, u32[]{:S(2)}) collective-permute-start(bf16[384,1536]{1,0:T(8,128)(2,1)} %pad_maximum_fusion.14), channel_id=1, source_target_pairs={{0,2},{2,0},{4,6},{6,4},{8,10},{10,8},{12,14},{14,12},{16,18},{18,... | collective-permute-start | bytes 3538952 | tf_op jit(solution)/shard_map/ppermute | solution.py:285
  (162 other events, 1090.6 us)

commit v2 on v1

--- a/solution.py
+++ b/solution.py
@@ -10,6 +10,16 @@
 SCALE_BITS = 27
 STEP = 2.0**11
 VM = 56 * 2**20
+SAME = 2**17
+
+
+def encode(buckets, same):
+    seq, hor, ver = buckets
+    return seq + 32 * hor + 2048 * ver + jnp.where(same, SAME, 0)
+
+
+def buckets_of(code):
+    return code & 31, (code >> 5) & 63, (code >> 11) & 63
 
 
 def dot_nt(a, b):
@@ -38,9 +48,73 @@
     return jnp.concatenate([jnp.where(lane < 64, x, zero), jnp.where(lane < 64, zero, x)], axis=0)
 
 
-def fwd_kernel(off, seq, hor, ver, formc, formr, tab, q, kt, v, p_out, c_out, b_ref, *, pairs, qb):
+def partner(axis, bit):
+    i = lax.axis_index(axis)
+    low = lax.rem(lax.div(i, bit), 2)
+    return {axis: i + bit * (1 - 2 * low)}
+
+
+def dp_bit(bit):
+    return lax.rem(lax.div(lax.axis_index("dp"), bit), 2)
+
+
+def greet(partners):
+    barrier = pltpu.get_barrier_semaphore()
+    for p in partners:
+        pl.semaphore_signal(barrier, inc=1, device_id=p, device_id_type=pl.DeviceIdType.MESH)
+    pl.semaphore_wait(barrier, len(partners))
+
+
+def remote(src, dst, send, recv, to):
+    return pltpu.make_async_remote_copy(
+        src_ref=src,
+        dst_ref=dst,
+        send_sem=send,
+        recv_sem=recv,
+        device_id=to,
+        device_id_type=pl.DeviceIdType.MESH,
+    )
+
+
+def fetch_hops(weights, others, send, recv):
+    hops = [[], [], []]
+    for n, (w, o) in enumerate(zip(weights, others)):
+        rows = w.shape[0] // 4
+        quarter = 2 * dp_bit(1) + dp_bit(2)
+        one = pl.ds(pl.multiple_of(quarter * rows, rows), rows)
+        two = pl.ds(pl.multiple_of(dp_bit(1) * (2 * rows), 2 * rows), 2 * rows)
+        hops[0].append(remote(w.at[one], o.at[one], send.at[n, 0], recv.at[n, 0], partner("head", 1)))
+        hops[1].append(remote(o.at[one], o.at[one], send.at[n, 1], recv.at[n, 1], partner("dp", 2)))
+        hops[2].append(remote(o.at[two], o.at[two], send.at[n, 2], recv.at[n, 2], partner("dp", 1)))
+    return hops
+
+
+def fwd_kernel(*refs, pairs, qb, n_fetch, steps):
+    code, tab, q, kt, v = refs[:5]
+    weights = refs[5 : 5 + n_fetch]
+    p_out, c_out = refs[5 + n_fetch : 7 + n_fetch]
+    others = refs[7 + n_fetch : 7 + 2 * n_fetch]
+    b_ref, send, recv = refs[7 + 2 * n_fetch :]
     keys = v.shape[0]
     chunk = 128
+    step = pl.program_id(0)
+    hops = fetch_hops(weights, others, send, recv)
+    at = [0, steps // 2, (3 * steps) // 4]
+
+    @pl.when(step == 0)
+    def _():
+        greet([partner("head", 1), partner("dp", 2), partner("dp", 1)])
+        for copy in hops[0]:
+            copy.start()
+
+    for hop in (1, 2):
+
+        @pl.when(step == at[hop])
+        def _():
+            for before, copy in zip(hops[hop - 1], hops[hop]):
+                before.wait_recv()
+                copy.start()
+
     tbs = [jnp.broadcast_to(tab[i : i + 1, :], (8, chunk)) for i in range(3 * pairs)]
 
     def gather(r, _):
@@ -48,8 +122,7 @@
         for c in range(keys // chunk):
             ls = slice(c * chunk, (c + 1) * chunk)
             sums = [None] * pairs
-            for t, b in enumerate((seq, hor, ver)):
-                idx = b[rs, ls]
+            for t, idx in enumerate(buckets_of(code[rs, ls])):
                 for j in range(pairs):
                     g = jnp.take_along_axis(tbs[3 * j + t], idx, axis=1, mode="promise_in_bounds")
                     sums[j] = g if t == 0 else sums[j] + g
@@ -58,7 +131,7 @@
         return 0
 
     lax.fori_loop(0, qb // 8, gather, 0)
-    same = formc[...] == formr[...]
+    same = code[...] >= SAME
     for j in range(pairs):
         lanes = slice(j * 128, (j + 1) * 128)
         q2 = split_pair(q[:, lanes])
@@ -76,42 +149,56 @@
         lane = lax.broadcasted_iota(I32, c0.shape, 1)
         c_out[:, lanes] = jnp.where(lane < 64, c0, c1).astype(BF16)
 
-
-def attend_fwd(off, buckets, formc, formr, tab, q, kt, v, qb=128):
+    @pl.when(step == steps - 1)
+    def _():
+        for copy in hops[2]:
+            copy.wait_recv()
+        for hop in hops:
+            for copy in hop:
+                copy.wait_send()
+
+
+def attend_fwd(code, tab, q, kt, v, weights, collective_id, qb=128):
     nq, width = q.shape
     keys = v.shape[0]
     pairs = width // 128
-    bspec = pl.BlockSpec((qb, keys), lambda i, off: (i + off[0], 0))
-    full = lambda a: pl.BlockSpec(a.shape, lambda i, off: (0,) * a.ndim)
+    n = len(weights)
+    steps = nq // qb
+    full = lambda a: pl.BlockSpec(a.shape, lambda i: (0,) * a.ndim)
+    anywhere = pl.BlockSpec(memory_space=pl.ANY)
     return pl.pallas_call(
-        functools.partial(fwd_kernel, pairs=pairs, qb=qb),
+        functools.partial(fwd_kernel, pairs=pairs, qb=qb, n_fetch=n, steps=steps),
         out_shape=(
             jax.ShapeDtypeStruct((2 * pairs, nq, keys), BF16),
             jax.ShapeDtypeStruct((nq, width), BF16),
+        )
+        + tuple(jax.ShapeDtypeStruct(w.shape, w.dtype) for w in weights),
+        grid=(steps,),
+        in_specs=[
+            pl.BlockSpec((qb, keys), lambda i: (i, 0)),
+            full(tab),
+            pl.BlockSpec((qb, width), lambda i: (i, 0)),
+            full(kt),
+            full(v),
+        ]
+        + [anywhere] * n,
+        out_specs=(
+            pl.BlockSpec((2 * pairs, qb, keys), lambda i: (0, i, 0)),
+            pl.BlockSpec((qb, width), lambda i: (i, 0)),
+        )
+        + (anywhere,) * n,
+        scratch_shapes=[
+            pltpu.VMEM((pairs, qb, keys), I32),
+            pltpu.SemaphoreType.DMA((n, 3)),
+            pltpu.SemaphoreType.DMA((n, 3)),
+        ],
+        compiler_params=pltpu.CompilerParams(
+            vmem_limit_bytes=VM, collective_id=collective_id, has_side_effects=True
         ),
-        grid_spec=pltpu.PrefetchScalarGridSpec(
-            num_scalar_prefetch=1,
-            grid=(nq // qb,),
-            in_specs=[bspec] * 3
-            + [
-                pl.BlockSpec((qb, 1), lambda i, off: (i + off[0], 0)),
-                full(formr),
-                full(tab),
-                pl.BlockSpec((qb, width), lambda i, off: (i, 0)),
-                full(kt),
-                full(v),
-            ],
-            out_specs=(
-                pl.BlockSpec((2 * pairs, qb, keys), lambda i, off: (0, i, 0)),
-                pl.BlockSpec((qb, width), lambda i, off: (i, 0)),
-            ),
-            scratch_shapes=[pltpu.VMEM((pairs, qb, keys), I32)],
+        cost_estimate=pl.CostEstimate(
+            flops=4 * nq * keys * width, bytes_accessed=90 * 2**20, transcendentals=nq * keys * 2 * pairs
         ),
-        compiler_params=pltpu.CompilerParams(vmem_limit_bytes=VM),
-        cost_estimate=pl.CostEstimate(
-            flops=4 * nq * keys * width, bytes_accessed=16 * 2**20, transcendentals=nq * keys * 2 * pairs
-        ),
-    )(off, *buckets, formc, formr, tab, q, kt, v)
+    )(code, tab, q, kt, v, *weights)
 
 
 def bwd_kernel(q, k, vt, do, p, ds_out, dq_out, dk_out, dv_out, *, pairs, qb):
@@ -169,11 +256,9 @@
     )(q, k, vt, do, p)
 
 
-def hist_kernel(off, seq, hor, ver, dsa, dsb, seq_out, hor_out, ver_out, rhs_ref, *, qb, bits):
-    keys = seq.shape[1]
-    heads = (dsa.shape[0], dsb.shape[0])
-    nh = sum(heads)
+def hist_kernel(code, dsa, dsb, seq_out, hor_out, ver_out, *, qb, bits):
     outs = (seq_out, hor_out, ver_out)
+    heads = dsa.shape[0]
 
     @pl.when(pl.program_id(0) == 0)
     def _():
@@ -182,12 +267,14 @@
 
     def rows(r, _):
         rs = pl.ds(pl.multiple_of(r * 16, 16), 16)
-        dfull = [d[h, rs, :].astype(F32) for d, n in ((dsa, heads[0]), (dsb, heads[1])) for h in range(n)]
+        dfull = [d[h, rs, :].astype(F32) for d in (dsa, dsb) for h in range(heads)]
         for half in range(2):
             d8 = [d[half * 8 : half * 8 + 8] for d in dfull]
-            for t, b in enumerate((seq, hor, ver)):
-                idx = b[pl.ds(pl.multiple_of(r * 16 + half * 8, 8), 8), :]
-                signs = [(((idx << (31 - i)) >> 31) | 1).astype(F32) for i in range(bits[t])]
+            packed = code[pl.ds(pl.multiple_of(r * 16 + half * 8, 8), 8), :]
+            low = 0
+            for t in range(3):
+                signs = [(((packed << (31 - low - i)) >> 31) | 1).astype(F32) for i in range(bits[t])]
+                low += bits[t]
                 rhs = jnp.concatenate(
                     [jnp.concatenate([d, d * signs[0]], axis=0).astype(BF16) for d in d8], axis=0
                 )
@@ -203,27 +290,22 @@
     lax.fori_loop(0, qb // 16, rows, 0)
 
 
-def hist(off, buckets, dsa, dsb, bits, qb=128):
+def hist(code, dsa, dsb, bits, qb=128):
     nq, keys = dsa.shape[1], dsa.shape[2]
     nh = dsa.shape[0] + dsb.shape[0]
-    bspec = pl.BlockSpec((qb, keys), lambda i, off: (i + off[0], 0))
     shapes = [(2 ** (b - 1) * 8, nh * 16) for b in bits]
     return pl.pallas_call(
         functools.partial(hist_kernel, qb=qb, bits=bits),
         out_shape=tuple(jax.ShapeDtypeStruct(s, F32) for s in shapes),
-        grid_spec=pltpu.PrefetchScalarGridSpec(
-            num_scalar_prefetch=1,
-            grid=(nq // qb,),
-            in_specs=[bspec] * 3
-            + [pl.BlockSpec((d.shape[0], qb, keys), lambda i, off: (0, i, 0)) for d in (dsa, dsb)],
-            out_specs=tuple(pl.BlockSpec(s, lambda i, off: (0, 0)) for s in shapes),
-            scratch_shapes=[pltpu.VMEM((nh * 16, keys), BF16)],
-        ),
+        grid=(nq // qb,),
+        in_specs=[pl.BlockSpec((qb, keys), lambda i: (i, 0))]
+        + [pl.BlockSpec((d.shape[0], qb, keys), lambda i: (0, i, 0)) for d in (dsa, dsb)],
+        out_specs=tuple(pl.BlockSpec(s, lambda i: (0, 0)) for s in shapes),
         compiler_params=pltpu.CompilerParams(vmem_limit_bytes=VM),
         cost_estimate=pl.CostEstimate(
-            flops=2 * nq * keys * 160 * nh * 8, bytes_accessed=20 * 2**20, transcendentals=0
+            flops=2 * nq * keys * 160 * nh * 8, bytes_accessed=110 * 2**20, transcendentals=0
         ),
-    )(off, *buckets, dsa, dsb)
+    )(code, dsa, dsb)
 
 
 def unhist(acc, bits, nh):
@@ -309,14 +391,6 @@
 
 def rows_of(x, index, rows):
     return lax.dynamic_slice_in_dim(x, index * rows, rows, 0)
-
-
-def fetch_other(w):
-    rows = w.shape[0] // 4
-    c, x = bit_of(1), bit_of(2)
-    mine = swap_head(rows_of(w, 2 * c + x, rows))
-    half = in_order(x, mine, swap_dp(mine, 2))
-    return in_order(c, half, swap_dp(half, 1))
 
 
 def halve(g, bit):
@@ -387,7 +461,6 @@
     head_index = lax.axis_index("head")
     share_start = head_index * share_rows
     block_rows = 128
-    off = jnp.full((1,), head_index * (share_rows // block_rows), I32)
     buckets = (sequence_bucket, horizontal_bucket, vertical_bucket)
     tables = (sequence_table, horizontal_table, vertical_table)
     bits = tuple((t.shape[0] - 1).bit_length() for t in tables)
@@ -396,33 +469,28 @@
     small = jnp.concatenate(
         [query_bias, value_bias, up_bias] + [t.reshape(-1) for t in tables]
     ).reshape(1, -1)
-    project_weights = (flat_project, fetch_other(flat_project))
     small_other = swap_head(small)[0]
-    output_weights = (output_weight, fetch_other(output_weight))
-    up_weights = (up_weight, fetch_other(up_weight))
-    down_weights = (down_weight, fetch_other(down_weight))
     cuts = [local_width, 2 * local_width, 2 * local_width + hidden]
-    ends = []
     for t in tables:
-        ends.append(cuts[-1] + t.size)
-        cuts.append(ends[-1])
-    other_query_bias = small_other[: cuts[0]]
-    other_value_bias = small_other[cuts[0] : cuts[1]]
-    other_up_bias = small_other[cuts[1] : cuts[2]]
+        cuts.append(cuts[-1] + t.size)
     other_tables = tuple(
         small_other[cuts[2 + i] : cuts[3 + i]].reshape(t.shape) for i, t in enumerate(tables)
     )
-    query_biases = (query_bias, other_query_bias)
-    value_biases = (value_bias, other_value_bias)
-    up_biases = (up_bias, other_up_bias)
+    query_biases = (query_bias, small_other[: cuts[0]])
+    value_biases = (value_bias, small_other[cuts[0] : cuts[1]])
+    up_biases = (up_bias, small_other[cuts[1] : cuts[2]])
     packed_tables = (pack_tables(tables), pack_tables(other_tables))
-
-    form_row = form_number.reshape(1, total_rows)
-    form_column = form_number.reshape(total_rows, 1)
+    project_weights = [flat_project]
+    output_weights, up_weights, down_weights = [output_weight], [up_weight], [down_weight]
+
+    form_row = form_number.reshape(total_rows)
+    form_own = lax.dynamic_slice_in_dim(form_row, share_start, share_rows, 0)
+    code = encode(
+        [rows_of(b, head_index, share_rows) for b in buckets], form_own[:, None] == form_row[None, :]
+    )
     own_tokens = rows_of(tokens, head_index, share_rows)
 
     scaled, keys, values_t, probs, contexts = [], [], [], [], []
-    attend = output_bias.astype(F32)
     for s in range(2):
         wq = project_weights[s][:, :local_width]
         wk = project_weights[s][:, local_width : 2 * local_width]
@@ -434,15 +502,22 @@
         kt = dot_general_t(wk, tokens).astype(BF16)
         v = (mm(tokens, wv) + bv).astype(BF16)
         vt = (dot_general_t(wv, tokens) + bv[:, None]).astype(BF16)
-        p, context = attend_fwd(
-            off, buckets, form_column, form_row, packed_tables[s], q, kt, v, qb=block_rows
+        fetch = (output_weight, up_weight, down_weight) if s else (flat_project,)
+        p, context, *fetched = attend_fwd(
+            code, packed_tables[s], q, kt, v, fetch, s, qb=block_rows
         )
-        attend = attend + mm(context, output_weights[s])
+        if s:
+            output_weights.append(fetched[0])
+            up_weights.append(fetched[1])
+            down_weights.append(fetched[2])
+        else:
+            project_weights.append(fetched[0])
         scaled.append(q)
         keys.append(k)
         values_t.append(vt)
         probs.append(p)
         contexts.append(context)
+    attend = output_bias.astype(F32) + sum(mm(contexts[s], output_weights[s]) for s in range(2))
     n1, root1 = normalize(own_tokens.astype(F32) + attend)
     normed = n1 * first_gain.astype(F32) + first_shift.astype(F32)
     normed_low = normed.astype(BF16)
@@ -513,7 +588,7 @@
     project_total = reduce_grad(project_grads[0], project_grads[1], True).reshape(
         model_width, 3, local_width
     )
-    counts = hist(off, buckets, back_scores[0], back_scores[1], bits, qb=block_rows)
+    counts = hist(code, back_scores[0], back_scores[1], bits, qb=block_rows)
     table_parts = [unhist(a, b, 2 * local_heads) for a, b in zip(counts, bits)]
 
     common = [

time: 589 us -> 558 us (0.947)
  waiting for transfers between devices: 163 us -> 128 us
  Pallas kernels: 114 us -> 146 us
  other arithmetic: 88.1 us -> 68.7 us
  starting transfers between devices: 51.5 us -> 45.6 us
    pallas_call x2, Pallas kernels: 54.1 us -> 85.8 us  [attend_fwd(): pl.pallas_call(functools.partial(fwd_kernel, pairs=pairs, qb=qb, n_fetch=...]
    ppermute x49 -> x41, waiting for transfers between devices: 130 us -> 99 us  [swap_dp(): return lax.ppermute(x, 'dp', [(i, i ^ bit) for i in range(n)])]
    select_n x23 -> x16, other arithmetic: 15.6 us -> 6.17 us  [in_order(): low = jnp.where(first == 0, mine, theirs)]
    dynamic_slice x27 -> x22, local copies, waits for them, and re-layouts: 19.8 us -> 13.7 us  [rows_of(): return lax.dynamic_slice_in_dim(x, index * rows, rows, 0)]
    ppermute x49 -> x41, starting transfers between devices: 39.8 us -> 34.7 us  [swap_dp(): return lax.ppermute(x, 'dp', [(i, i ^ bit) for i in range(n)])]
    ppermute x11 -> x7, waiting for transfers between devices: 32.4 us -> 28.9 us  [swap_head(): return lax.ppermute(x, 'head', [(0, 1), (1, 0)])]
    unnamed x290 -> x238, local copies, waits for them, and re-layouts: 26.3 us -> 23.8 us
    ppermute x11 -> x7, starting transfers between devices: 11.8 us -> 10.9 us  [swap_head(): return lax.ppermute(x, 'head', [(0, 1), (1, 0)])]
  transfers between devices with their start and end apart: 60 -> 48, of which waited for: 25 -> 21; matrix products, arithmetic and copies ran while one was open for 29% -> 24% of each run, Pallas kernels for 15% -> 12%
where the time goes in v2:
time: 558 us; the launch traced here: 547 us
  Pallas kernels  146 us (26%)
  waiting for transfers between devices  128 us (23%)
  matrix products  81.9 us (15%)
  local copies, waits for them, and re-layouts  74.9 us (13%)
  other arithmetic  68.7 us (12%)
  starting transfers between devices  45.6 us (8%)
    ppermute x41, waiting for transfers between devices, swap_dp(): return lax.ppermute(x, 'dp', [(i, i ^ bit) for i in range(n)])  99 us
    pallas_call x2, Pallas kernels, attend_fwd(): pl.pallas_call(functools.partial(fwd_kernel, pairs=pairs, qb=qb, n_fetch=...  85.8 us
    ppermute x41, starting transfers between devices, swap_dp(): return lax.ppermute(x, 'dp', [(i, i ^ bit) for i in range(n)])  34.7 us
    pallas_call x1, Pallas kernels, hist(): pl.pallas_call(functools.partial(hist_kernel, qb=qb, bits=bits), out_shap...  34.1 us
    ppermute x7, waiting for transfers between devices, swap_head(): return lax.ppermute(x, 'head', [(0, 1), (1, 0)])  28.9 us
    pallas_call x2, Pallas kernels, attend_bwd(): pl.pallas_call(functools.partial(bwd_kernel, pairs=pairs, qb=qb), out_sha...  25.8 us
    unnamed x238, local copies, waits for them, and re-layouts  23.8 us
    dot_general x11, matrix products, mm(): return jnp.dot(a, b, preferred_element_type=F32)  23.1 us
  transfers between devices with their start and end apart: 48, of which 21 were waited for; matrix products, arithmetic and copies ran while one was open for 24% of the time, Pallas kernels for 12%

profile of v2, /device:TPU:0, one launch (start us, length us, event | category | flops | bytes accessed | tf_op | source)
XLA Modules:
  0.0 547.4 jit_solution(13254237977683503694)
XLA Ops:
  5.6 3.0 collective-permute-start
  28.2 4.7 select_add_fusion.refs_0_.code
  32.9 33.1 %shard_map.621 = (bf16[6,512,1024]{2,1,0:T(8,128)(2,1)}, bf16[512,384]{1,0:T(8,128)(2,1)}, bf16[768,1152]{1,0:T(8,128)(2,1)}) custom-call(s32[512,1024]{1,0:T(8,128)} %select_add_fusion.refs_0_.code, s32[9,128]{1,0:T(8,128)} %add.580.refs_1_, bf16[512,384]{1,0:T(8,128)(2,1)} %fusion.18.refs_2_.q, bf16[384,1024]{1,0:T(8,128)(2,1)} %convolution_convert_fusion.6.refs_3_, ...), custom_call_target="tpu_custom_call" | custom-call | flops 805306368 | bytes 94371840 | tf_op jit(solution)/shard_map/pallas_call | solution.py:169
  66.1 3.0 convolution_convert_fusion.4
  81.3 4.5 concatenate.96
  95.2 52.7 %shard_map.622 = (bf16[6,512,1024]{2,1,0:T(8,128)(2,1)}, bf16[512,384]{1,0:T(8,128)(2,1)}, bf16[384,768]{1,0:T(8,128)(2,1)}, bf16[768,1536]{1,0:T(8,128)(2,1)}, bf16[1536,768]{1,0:T(8,128)(2,1)}) custom-call(s32[512,1024]{1,0:T(8,128)} %select_add_fusion.refs_0_.code, s32[9,128]{1,0:T(8,128)} %add.586.refs_1_, bf16[512,384]{1,0:T(8,128)(2,1)} %fusion.46.refs_2_.q, ...), custom_call_target="tpu_custom_call" | custom-call | flops 805306368 | bytes 94371840 | tf_op jit(solution)/shard_map/pallas_call | solution.py:169
  151.8 3.5 multiply_convert_fusion.1
  157.5 3.5 multiply_convert_fusion
  167.5 4.7 convert_reduce_fusion
  172.3 4.2 convert_reduce_fusion.1
  185.5 12.8 %shard_map.624 = (bf16[6,512,1024]{2,1,0:T(8,128)(2,1)}, bf16[512,384]{1,0:T(8,128)(2,1)}, f32[384,1024]{1,0:T(8,128)}, f32[384,1024]{1,0:T(8,128)}) custom-call(bf16[512,384]{1,0:T(8,128)(2,1)} %fusion.46.refs_2_.q, bf16[1024,384]{1,0:T(8,128)(2,1)} %bitcast.164, bf16[384,1024]{1,0:T(8,128)(2,1)} %add_convert_fusion.12.vt, ...), custom_call_target="tpu_custom_call" | custom-call | flops 1610612736 | bytes 31457280 | tf_op jit(solution)/shard_map/pallas_call | solution.py:241
  202.6 13.0 %shard_map.623 = (bf16[6,512,1024]{2,1,0:T(8,128)(2,1)}, bf16[512,384]{1,0:T(8,128)(2,1)}, f32[384,1024]{1,0:T(8,128)}, f32[384,1024]{1,0:T(8,128)}) custom-call(bf16[512,384]{1,0:T(8,128)(2,1)} %fusion.18.refs_2_.q, bf16[1024,384]{1,0:T(8,128)(2,1)} %convolution_convert_fusion.5.k, bf16[384,1024]{1,0:T(8,128)(2,1)} %add_convert_fusion.11.vt, ...), custom_call_target="tpu_custom_call" | custom-call | flops 1610612736 | bytes 31457280 | tf_op jit(solution)/shard_map/pallas_call | solution.py:241
  236.4 2.8 convolution_convert_fusion.3
  239.2 2.8 convolution_convert_fusion
  242.0 2.9 convolution_convert_fusion.1
  253.7 34.1 %shard_map.625 = (f32[128,192]{1,0:T(8,128)}, f32[256,192]{1,0:T(8,128)}, f32[256,192]{1,0:T(8,128)}) custom-call(s32[512,1024]{1,0:T(8,128)} %select_add_fusion.refs_0_.code, bf16[6,512,1024]{2,1,0:T(8,128)(2,1)} %get-tuple-element.67.dsa, bf16[6,512,1024]{2,1,0:T(8,128)(2,1)} %get-tuple-element.68.dsb), custom_call_target="tpu_custom_call" | custom-call | flops 16106127360 | bytes 115343360 | tf_op jit(solution)/shard_map/pallas_call | solution.py:297
  293.3 3.4 reshape.387
  326.1 5.5 %collective-permute-done.19 = bf16[192,768]{1,0:T(8,128)(2,1)} collective-permute-done((bf16[192,768]{1,0:T(8,128)(2,1)S(1)}, bf16[192,768]{1,0:T(8,128)(2,1)}, u32[]{:S(2)}, u32[]{:S(2)}) %collective-permute-start.19) | collective-permute-done | bytes 294944 | tf_op jit(solution)/shard_map/ppermute | solution.py:371
  360.6 5.4 convert_add_fusion
  369.7 2.9 collective-permute-done.25
  387.8 7.4 %collective-permute-done.4 = bf16[384,1152]{0,1:T(8,128)(2,1)S(1)} collective-permute-done((bf16[384,1152]{0,1:T(8,128)(2,1)S(1)}, bf16[384,1152]{0,1:T(8,128)(2,1)S(1)}, u32[]{:S(2)}, u32[]{:S(2)}) %collective-permute-start.4) | collective-permute-done | bytes 884768 | tf_op jit(solution)/shard_map/ppermute | solution.py:371
  402.7 13.0 %collective-permute-done.5 = bf16[192,1152]{1,0:T(8,128)(2,1)S(1)} collective-permute-done((bf16[192,1152]{1,0:T(8,128)(2,1)S(1)}, bf16[192,1152]{1,0:T(8,128)(2,1)S(1)}, u32[]{:S(2)}, u32[]{:S(2)}) %collective-permute-start.5) | collective-permute-done | bytes 442400 | tf_op jit(solution)/shard_map/ppermute | solution.py:367
  416.8 16.0 %collective-permute-done.31 = bf16[192,1536]{1,0:T(8,128)(2,1)} collective-permute-done((bf16[192,1536]{1,0:T(8,128)(2,1)}, bf16[192,1536]{1,0:T(8,128)(2,1)}, u32[]{:S(2)}, u32[]{:S(2)}) %collective-permute-start.31) | collective-permute-done | bytes 589856 | tf_op jit(solution)/shard_map/ppermute | solution.py:371
  437.1 13.7 %collective-permute-done.7 = bf16[48,1152]{0,1:T(8,128)(2,1)S(1)} collective-permute-done((bf16[48,1152]{0,1:T(8,128)(2,1)S(1)}, bf16[48,1152]{0,1:T(8,128)(2,1)S(1)}, u32[]{:S(2)}, u32[]{:S(2)}) %collective-permute-start.7) | collective-permute-done | bytes 110624 | tf_op jit(solution)/shard_map/ppermute | solution.py:367
  453.0 12.8 %collective-permute-done.8 = bf16[48,1152]{0,1:T(8,128)(2,1)S(1)} collective-permute-done((bf16[48,1152]{0,1:T(8,128)(2,1)S(1)}, bf16[48,1152]{0,1:T(8,128)(2,1)S(1)}, u32[]{:S(2)}, u32[]{:S(2)}) %collective-permute-start.8) | collective-permute-done | bytes 110624 | tf_op jit(solution)/shard_map/ppermute | solution.py:367
  466.3 6.5 %collective-permute-done.33 = bf16[48,1536]{1,0:T(8,128)(2,1)S(1)} collective-permute-done((bf16[48,1536]{1,0:T(8,128)(2,1)S(1)}, bf16[48,1536]{1,0:T(8,128)(2,1)S(1)}, u32[]{:S(2)}, u32[]{:S(2)}) %collective-permute-start.33) | collective-permute-done | bytes 147488 | tf_op jit(solution)/shard_map/ppermute | solution.py:367
  474.3 5.2 collective-permute-done.9
  486.2 7.7 %collective-permute-done.35 = bf16[96,1536]{1,0:T(8,128)(2,1)S(1)} collective-permute-done((bf16[96,1536]{1,0:T(8,128)(2,1)S(1)}, bf16[96,1536]{1,0:T(8,128)(2,1)S(1)}, u32[]{:S(2)}, u32[]{:S(2)}) %collective-permute-start.35) | collective-permute-done | bytes 294944 | tf_op jit(solution)/shard_map/ppermute | solution.py:367
  500.3 6.4 %collective-permute-done.43 = bf16[96,768]{1,0:T(8,128)(2,1)S(1)} collective-permute-done((bf16[96,768]{1,0:T(8,128)(2,1)S(1)}, bf16[96,768]{1,0:T(8,128)(2,1)S(1)}, u32[]{:S(2)}, u32[]{:S(2)}) %collective-permute-start.43) | collective-permute-done | bytes 147488 | tf_op jit(solution)/shard_map/ppermute | solution.py:367
  507.2 6.5 %collective-permute-done.44 = bf16[96,768]{1,0:T(8,128)(2,1)S(1)} collective-permute-done((bf16[96,768]{1,0:T(8,128)(2,1)S(1)}, bf16[96,768]{1,0:T(8,128)(2,1)S(1)}, u32[]{:S(2)}, u32[]{:S(2)}) %collective-permute-start.44) | collective-permute-done | bytes 147488 | tf_op jit(solution)/shard_map/ppermute | solution.py:367
  515.2 7.0 %collective-permute-done.45 = bf16[192,768]{1,0:T(8,128)(2,1)S(1)} collective-permute-done((bf16[192,768]{1,0:T(8,128)(2,1)S(1)}, bf16[192,768]{1,0:T(8,128)(2,1)S(1)}, u32[]{:S(2)}, u32[]{:S(2)}) %collective-permute-start.45) | collective-permute-done | bytes 294944 | tf_op jit(solution)/shard_map/ppermute | solution.py:367
  531.7 5.5 collective-permute-done.46
  (565 shorter events, 234.5 us)
Async XLA Ops:
  5.6 80.1 %collective-permute-start = (bf16[1,3264]{1,0:T(2,128)(2,1)S(1)}, bf16[1,3264]{1,0:T(2,128)(2,1)S(1)}, u32[]{:S(2)}, u32[]{:S(2)}) collective-permute-start(bf16[1,3264]{1,0:T(2,128)(2,1)S(1)} %reshape.384), channel_id=1, source_target_pairs={{0,1},{1,0},{2,3},{3,2},{4,5},{5,4},{6,7},{7,6},{8,9},{9,8},{10,11... | collective-permute-start | bytes 19592 | tf_op jit(solution)/shard_map/ppermute | solution.py:371
  248.4 109.7 %collective-permute-start.1 = (bf16[512,768]{1,0:T(8,128)(2,1)}, bf16[512,768]{1,0:T(8,128)(2,1)}, u32[]{:S(2)}, u32[]{:S(2)}) collective-permute-start(bf16[512,768]{1,0:T(8,128)(2,1)} %add_convert_fusion.10), channel_id=1, source_target_pairs={{0,1},{1,0},{2,3},{3,2},{4,5},{5,4},{6,7},{7,6},{8,9},{9,8},{10,11... | collective-permute-start | bytes 2359304 | tf_op jit(solution)/shard_map/ppermute | solution.py:371
  251.5 115.0 %collective-permute-start.3 = (bf16[384,1152]{0,1:T(8,128)(2,1)}, bf16[384,1152]{0,1:T(8,128)(2,1)}, u32[]{:S(2)}, u32[]{:S(2)}) collective-permute-start(bf16[384,1152]{0,1:T(8,128)(2,1)} %constant_dynamic-slice_fusion.19), channel_id=1, source_target_pairs={{0,2},{2,0},{4,6},{6,4},{8,10},{10,8},{12,14},{14,12},{16,18},{18,... | collective-permute-start | bytes 2654216 | tf_op jit(solution)/shard_map/ppermute | solution.py:367
  253.5 133.8 %collective-permute-start.2 = (bf16[384,1152]{0,1:T(8,128)(2,1)}, bf16[384,1152]{0,1:T(8,128)(2,1)}, u32[]{:S(2)}, u32[]{:S(2)}) collective-permute-start(bf16[384,1152]{0,1:T(8,128)(2,1)} %constant_dynamic-slice_fusion.20), channel_id=1, source_target_pairs={{0,2},{2,0},{4,6},{6,4},{8,10},{10,8},{12,14},{14,12},{16,18},{18,... | collective-permute-start | bytes 2654216 | tf_op jit(solution)/shard_map/ppermute | solution.py:367
  301.9 19.9 %collective-permute-start.18 = (bf16[192,768]{1,0:T(8,128)(2,1)S(1)}, bf16[192,768]{1,0:T(8,128)(2,1)S(1)}, u32[]{:S(2)}, u32[]{:S(2)}) collective-permute-start(bf16[192,768]{1,0:T(8,128)(2,1)S(1)} %constant_dynamic-slice_fusion.14), channel_id=1, source_target_pairs={{0,2},{2,0},{4,6},{6,4},{8,10},{10,8},{12,14},{14,12},{16,18},{18,... | collective-permute-start | bytes 884744 | tf_op jit(solution)/shard_map/ppermute | solution.py:367
  321.9 9.6 %collective-permute-start.19 = (bf16[192,768]{1,0:T(8,128)(2,1)S(1)}, bf16[192,768]{1,0:T(8,128)(2,1)}, u32[]{:S(2)}, u32[]{:S(2)}) collective-permute-start(bf16[192,768]{1,0:T(8,128)(2,1)S(1)} %add_convert_fusion.22), channel_id=1, source_target_pairs={{0,1},{1,0},{2,3},{3,2},{4,5},{5,4},{6,7},{7,6},{8,9},{9,8},{10,11... | collective-permute-start | bytes 884744 | tf_op jit(solution)/shard_map/ppermute | solution.py:371
  325.8 46.8 %collective-permute-start.29 = (bf16[384,1536]{1,0:T(8,128)(2,1)}, bf16[384,1536]{1,0:T(8,128)(2,1)}, u32[]{:S(2)}, u32[]{:S(2)}) collective-permute-start(bf16[384,1536]{1,0:T(8,128)(2,1)} %constant_dynamic-slice_fusion.8), channel_id=1, source_target_pairs={{0,2},{2,0},{4,6},{6,4},{8,10},{10,8},{12,14},{14,12},{16,18},{18,... | collective-permute-start | bytes 3538952 | tf_op jit(solution)/shard_map/ppermute | solution.py:367
  347.9 10.2 %collective-permute-start.23 = (bf16[24,768]{1,0:T(8,128)(2,1)S(1)}, bf16[24,768]{1,0:T(8,128)(2,1)S(1)}, u32[]{:S(2)}, u32[]{:S(2)}) collective-permute-start(bf16[24,768]{1,0:T(8,128)(2,1)S(1)} %add_convert_fusion.30), channel_id=1, source_target_pairs={{0,16},{2,18},{4,20},{6,22},{8,24},{10,26},{12,28},{14,30},{16,0},... | collective-permute-start | bytes 110600 | tf_op jit(solution)/shard_map/ppermute | solution.py:367
  358.1 18.8 %collective-permute-start.27 = (bf16[384,1536]{1,0:T(8,128)(2,1)}, bf16[384,1536]{1,0:T(8,128)(2,1)S(1)}, u32[]{:S(2)}, u32[]{:S(2)}) collective-permute-start(bf16[384,1536]{1,0:T(8,128)(2,1)} %constant_dynamic-slice_fusion.10), channel_id=1, source_target_pairs={{0,2},{2,0},{4,6},{6,4},{8,10},{10,8},{12,14},{14,12},{16,18},{18,... | collective-permute-start | bytes 3538952 | tf_op jit(solution)/shard_map/ppermute | solution.py:367
  366.1 11.7 %collective-permute-start.39 = (bf16[768,768]{1,0:T(8,128)(2,1)S(1)}, bf16[768,768]{1,0:T(8,128)(2,1)S(1)}, u32[]{:S(2)}, u32[]{:S(2)}) collective-permute-start(bf16[768,768]{1,0:T(8,128)(2,1)S(1)} %copy-done.39), channel_id=1, source_target_pairs={{0,2},{2,0},{4,6},{6,4},{8,10},{10,8},{12,14},{14,12},{16,18},{18,... | collective-permute-start | bytes 3538952 | tf_op jit(solution)/shard_map/ppermute | solution.py:367
  372.6 62.4 %collective-permute-start.38 = (bf16[768,768]{1,0:T(8,128)(2,1)}, bf16[768,768]{1,0:T(8,128)(2,1)}, u32[]{:S(2)}, u32[]{:S(2)}) collective-permute-start(bf16[768,768]{1,0:T(8,128)(2,1)} %constant_dynamic-slice_fusion.4), channel_id=1, source_target_pairs={{0,2},{2,0},{4,6},{6,4},{8,10},{10,8},{12,14},{14,12},{16,18},{18,... | collective-permute-start | bytes 3538952 | tf_op jit(solution)/shard_map/ppermute | solution.py:367
  372.7 22.5 %collective-permute-start.4 = (bf16[384,1152]{0,1:T(8,128)(2,1)S(1)}, bf16[384,1152]{0,1:T(8,128)(2,1)S(1)}, u32[]{:S(2)}, u32[]{:S(2)}) collective-permute-start(bf16[384,1152]{0,1:T(8,128)(2,1)S(1)} %add_convert_fusion.8), channel_id=1, source_target_pairs={{0,1},{1,0},{2,3},{3,2},{4,5},{5,4},{6,7},{7,6},{8,9},{9,8},{10,11... | collective-permute-start | bytes 2654216 | tf_op jit(solution)/shard_map/ppermute | solution.py:371
  377.8 21.3 %collective-permute-start.30 = (bf16[192,1536]{1,0:T(8,128)(2,1)}, bf16[192,1536]{1,0:T(8,128)(2,1)}, u32[]{:S(2)}, u32[]{:S(2)}) collective-permute-start(bf16[192,1536]{1,0:T(8,128)(2,1)} %constant_dynamic-slice_fusion.7), channel_id=1, source_target_pairs={{0,4},{2,6},{4,0},{6,2},{8,12},{10,14},{12,8},{14,10},{16,20},{18,... | collective-permute-start | bytes 1769480 | tf_op jit(solution)/shard_map/ppermute | solution.py:367
  381.8 35.0 %collective-permute-start.28 = (bf16[192,1536]{1,0:T(8,128)(2,1)}, bf16[192,1536]{1,0:T(8,128)(2,1)}, u32[]{:S(2)}, u32[]{:S(2)}) collective-permute-start(bf16[192,1536]{1,0:T(8,128)(2,1)} %constant_dynamic-slice_fusion.9), channel_id=1, source_target_pairs={{0,4},{2,6},{4,0},{6,2},{8,12},{10,14},{12,8},{14,10},{16,20},{18,... | collective-permute-start | bytes 1769480 | tf_op jit(solution)/shard_map/ppermute | solution.py:367
  387.2 47.8 %collective-permute-start.40 = (bf16[768,768]{1,0:T(8,128)(2,1)}, bf16[768,768]{1,0:T(8,128)(2,1)}, u32[]{:S(2)}, u32[]{:S(2)}) collective-permute-start(bf16[768,768]{1,0:T(8,128)(2,1)} %add_convert_fusion.3), channel_id=1, source_target_pairs={{0,1},{1,0},{2,3},{3,2},{4,5},{5,4},{6,7},{7,6},{8,9},{9,8},{10,11... | collective-permute-start | bytes 3538952 | tf_op jit(solution)/shard_map/ppermute | solution.py:371
  397.2 18.5 %collective-permute-start.5 = (bf16[192,1152]{1,0:T(8,128)(2,1)S(1)}, bf16[192,1152]{1,0:T(8,128)(2,1)S(1)}, u32[]{:S(2)}, u32[]{:S(2)}) collective-permute-start(bf16[192,1152]{1,0:T(8,128)(2,1)S(1)} %copy.139), channel_id=1, source_target_pairs={{0,4},{2,6},{4,0},{6,2},{8,12},{10,14},{12,8},{14,10},{16,20},{18,... | collective-permute-start | bytes 1327112 | tf_op jit(solution)/shard_map/ppermute | solution.py:367
  401.1 31.8 %collective-permute-start.31 = (bf16[192,1536]{1,0:T(8,128)(2,1)}, bf16[192,1536]{1,0:T(8,128)(2,1)}, u32[]{:S(2)}, u32[]{:S(2)}) collective-permute-start(bf16[192,1536]{1,0:T(8,128)(2,1)} %add_convert_fusion.16), channel_id=1, source_target_pairs={{0,1},{1,0},{2,3},{3,2},{4,5},{5,4},{6,7},{7,6},{8,9},{9,8},{10,11... | collective-permute-start | bytes 1769480 | tf_op jit(solution)/shard_map/ppermute | solution.py:371
  416.7 17.9 %collective-permute-start.6 = (bf16[96,1152]{0,1:T(8,128)(2,1)S(1)}, bf16[96,1152]{0,1:T(8,128)(2,1)S(1)}, u32[]{:S(2)}, u32[]{:S(2)}) collective-permute-start(bf16[96,1152]{0,1:T(8,128)(2,1)S(1)} %constant_dynamic-slice_fusion.17), channel_id=1, source_target_pairs={{0,8},{2,10},{4,12},{6,14},{8,0},{10,2},{12,4},{14,6},{16,24},{18,... | collective-permute-start | bytes 663560 | tf_op jit(solution)/shard_map/ppermute | solution.py:367
  434.5 31.3 %collective-permute-start.32 = (bf16[96,1536]{1,0:T(8,128)(2,1)S(1)}, bf16[96,1536]{1,0:T(8,128)(2,1)S(1)}, u32[]{:S(2)}, u32[]{:S(2)}) collective-permute-start(bf16[96,1536]{1,0:T(8,128)(2,1)S(1)} %constant_dynamic-slice_fusion.6), channel_id=1, source_target_pairs={{0,8},{2,10},{4,12},{6,14},{8,0},{10,2},{12,4},{14,6},{16,24},{18,... | collective-permute-start | bytes 884744 | tf_op jit(solution)/shard_map/ppermute | solution.py:367
  434.9 15.9 %collective-permute-start.7 = (bf16[48,1152]{0,1:T(8,128)(2,1)S(1)}, bf16[48,1152]{0,1:T(8,128)(2,1)S(1)}, u32[]{:S(2)}, u32[]{:S(2)}) collective-permute-start(bf16[48,1152]{0,1:T(8,128)(2,1)S(1)} %constant_dynamic-slice_fusion.16), channel_id=1, source_target_pairs={{0,16},{2,18},{4,20},{6,22},{8,24},{10,26},{12,28},{14,30},{16,0},... | collective-permute-start | bytes 331784 | tf_op jit(solution)/shard_map/ppermute | solution.py:367
  451.0 14.8 %collective-permute-start.8 = (bf16[48,1152]{0,1:T(8,128)(2,1)S(1)}, bf16[48,1152]{0,1:T(8,128)(2,1)S(1)}, u32[]{:S(2)}, u32[]{:S(2)}) collective-permute-start(bf16[48,1152]{0,1:T(8,128)(2,1)S(1)} %add_convert_fusion.24), channel_id=1, source_target_pairs={{0,16},{2,18},{4,20},{6,22},{8,24},{10,26},{12,28},{14,30},{16,0},... | collective-permute-start | bytes 331784 | tf_op jit(solution)/shard_map/ppermute | solution.py:367
  451.1 32.8 %collective-permute-start.41 = (bf16[384,768]{1,0:T(8,128)(2,1)S(1)}, bf16[384,768]{1,0:T(8,128)(2,1)S(1)}, u32[]{:S(2)}, u32[]{:S(2)}) collective-permute-start(bf16[384,768]{1,0:T(8,128)(2,1)S(1)} %constant_dynamic-slice_fusion.2), channel_id=1, source_target_pairs={{0,4},{2,6},{4,0},{6,2},{8,12},{10,14},{12,8},{14,10},{16,20},{18,... | collective-permute-start | bytes 1769480 | tf_op jit(solution)/shard_map/ppermute | solution.py:367
  466.2 13.4 %collective-permute-start.9 = (bf16[96,1152]{0,1:T(8,128)(2,1)S(1)}, bf16[96,1152]{0,1:T(8,128)(2,1)S(1)}, u32[]{:S(2)}, u32[]{:S(2)}) collective-permute-start(bf16[96,1152]{0,1:T(8,128)(2,1)S(1)} %pad_maximum_fusion.8), channel_id=1, source_target_pairs={{0,8},{2,10},{4,12},{6,14},{8,0},{10,2},{12,4},{14,6},{16,24},{18,... | collective-permute-start | bytes 663560 | tf_op jit(solution)/shard_map/ppermute | solution.py:367
  473.5 9.3 %collective-permute-start.34 = (bf16[48,1536]{1,0:T(8,128)(2,1)}, bf16[48,1536]{1,0:T(8,128)(2,1)}, u32[]{:S(2)}, u32[]{:S(2)}) collective-permute-start(bf16[48,1536]{1,0:T(8,128)(2,1)} %add_convert_fusion.27), channel_id=1, source_target_pairs={{0,16},{2,18},{4,20},{6,22},{8,24},{10,26},{12,28},{14,30},{16,0},... | collective-permute-start | bytes 442376 | tf_op jit(solution)/shard_map/ppermute | solution.py:367
  481.1 17.6 %collective-permute-start.10 = (bf16[192,1152]{1,0:T(8,128)(2,1)}, bf16[192,1152]{1,0:T(8,128)(2,1)}, u32[]{:S(2)}, u32[]{:S(2)}) collective-permute-start(bf16[192,1152]{1,0:T(8,128)(2,1)} %copy.141), channel_id=1, source_target_pairs={{0,4},{2,6},{4,0},{6,2},{8,12},{10,14},{12,8},{14,10},{16,20},{18,... | collective-permute-start | bytes 1327112 | tf_op jit(solution)/shard_map/ppermute | solution.py:367
  483.9 10.0 %collective-permute-start.35 = (bf16[96,1536]{1,0:T(8,128)(2,1)S(1)}, bf16[96,1536]{1,0:T(8,128)(2,1)S(1)}, u32[]{:S(2)}, u32[]{:S(2)}) collective-permute-start(bf16[96,1536]{1,0:T(8,128)(2,1)S(1)} %pad_maximum_fusion.10), channel_id=1, source_target_pairs={{0,8},{2,10},{4,12},{6,14},{8,0},{10,2},{12,4},{14,6},{16,24},{18,... | collective-permute-start | bytes 884744 | tf_op jit(solution)/shard_map/ppermute | solution.py:367
  484.1 14.2 %collective-permute-start.42 = (bf16[192,768]{1,0:T(8,128)(2,1)S(1)}, bf16[192,768]{1,0:T(8,128)(2,1)S(1)}, u32[]{:S(2)}, u32[]{:S(2)}) collective-permute-start(bf16[192,768]{1,0:T(8,128)(2,1)S(1)} %constant_dynamic-slice_fusion.1), channel_id=1, source_target_pairs={{0,8},{2,10},{4,12},{6,14},{8,0},{10,2},{12,4},{14,6},{16,24},{18,... | collective-permute-start | bytes 884744 | tf_op jit(solution)/shard_map/ppermute | solution.py:367
  494.0 19.8 %collective-permute-start.36 = (bf16[192,1536]{1,0:T(8,128)(2,1)S(1)}, bf16[192,1536]{1,0:T(8,128)(2,1)S(1)}, u32[]{:S(2)}, u32[]{:S(2)}) collective-permute-start(bf16[192,1536]{1,0:T(8,128)(2,1)S(1)} %pad_maximum_fusion.6), channel_id=1, source_target_pairs={{0,4},{2,6},{4,0},{6,2},{8,12},{10,14},{12,8},{14,10},{16,20},{18,... | collective-permute-start | bytes 1769480 | tf_op jit(solution)/shard_map/ppermute | solution.py:367
  507.1 16.5 %collective-permute-start.11 = (bf16[384,1152]{0,1:T(8,128)(2,1)S(1)}, bf16[384,1152]{0,1:T(8,128)(2,1)S(1)}, u32[]{:S(2)}, u32[]{:S(2)}) collective-permute-start(bf16[384,1152]{0,1:T(8,128)(2,1)S(1)} %pad_maximum_fusion.4), channel_id=1, source_target_pairs={{0,2},{2,0},{4,6},{6,4},{8,10},{10,8},{12,14},{14,12},{16,18},{18,... | collective-permute-start | bytes 2654216 | tf_op jit(solution)/shard_map/ppermute | solution.py:367
  513.8 8.4 %collective-permute-start.45 = (bf16[192,768]{1,0:T(8,128)(2,1)S(1)}, bf16[192,768]{1,0:T(8,128)(2,1)S(1)}, u32[]{:S(2)}, u32[]{:S(2)}) collective-permute-start(bf16[192,768]{1,0:T(8,128)(2,1)S(1)} %pad_maximum_fusion.11), channel_id=1, source_target_pairs={{0,8},{2,10},{4,12},{6,14},{8,0},{10,2},{12,4},{14,6},{16,24},{18,... | collective-permute-start | bytes 884744 | tf_op jit(solution)/shard_map/ppermute | solution.py:367
  515.2 23.4 %collective-permute-start.37 = (bf16[384,1536]{1,0:T(8,128)(2,1)}, bf16[384,1536]{1,0:T(8,128)(2,1)}, u32[]{:S(2)}, u32[]{:S(2)}) collective-permute-start(bf16[384,1536]{1,0:T(8,128)(2,1)} %pad_maximum_fusion.2), channel_id=1, source_target_pairs={{0,2},{2,0},{4,6},{6,4},{8,10},{10,8},{12,14},{14,12},{16,18},{18,... | collective-permute-start | bytes 3538952 | tf_op jit(solution)/shard_map/ppermute | solution.py:367
  523.1 14.0 %collective-permute-start.46 = (bf16[384,768]{1,0:T(8,128)(2,1)}, bf16[384,768]{1,0:T(8,128)(2,1)}, u32[]{:S(2)}, u32[]{:S(2)}) collective-permute-start(bf16[384,768]{1,0:T(8,128)(2,1)} %pad_maximum_fusion.7), channel_id=1, source_target_pairs={{0,4},{2,6},{4,0},{6,2},{8,12},{10,14},{12,8},{14,10},{16,20},{18,... | collective-permute-start | bytes 1769480 | tf_op jit(solution)/shard_map/ppermute | solution.py:367
  (124 other events, 675.1 us)
